TPU v7x, 32 devices: a whole 2x2x4 slice. The times are simulated.
32 devices in a mesh: row: 4 (over y, x), col: 8 (over z, core).
Axes of the slice: x: 2, y: 2, z: 4, core: 2. Of those that a mesh axis runs over, the one named last changes fastest.
Arguments:
- features: bfloat16 [16384, 256], P(('col', 'row')), may hold values from -6 to 6
- weight: bfloat16 [256, 256], replicated, may hold values from -0.375 to 0.375
- tile_values: bfloat16 [16384, 128, 128], P(('row', 'col')), may hold values from -0.046875 to 0.046875
- tile_row: int32 [16384], P(('row', 'col')), may hold values from 0 to 31, as said below
- tile_col: int32 [16384], P(('row', 'col')), may hold values from 0 to 15, as said below
- tile_count: int32 [4, 8], P('row', 'col'), may hold values from 128 to 512, as said below
- cotangent: bfloat16 [16384, 256], P(('row', 'col')), may hold values from -6 to 6
Outputs:
- activated: bfloat16 [16384, 256], P(('row', 'col'))
- grad_features: bfloat16 [16384, 256], P(('col', 'row'))
- grad_weight: float32 [256, 256], replicated
Inputs may be any that keep to these rules, and one draw needn't show every extreme that they name: `tile_count`: 512 on at least one device in every draw. Within each device's slots the pairs (tile_row, tile_col) are distinct. Within each device's slots the pairs (tile_row, tile_col) are distinct.
All inputs are finite; a program needn't handle non-finite values.
Results may differ from a plain program's by a relative error of at most 0.024.
Values may be sent and summed in bfloat16 or wider, within the bound.
No kernel may reach another device: no remote copies, remote signals or barrier semaphores. Data moves between devices by JAX's collectives and lax.ppermute only.
A program may use at most 128 MiB of HBM per device.

v0:
```python
import math

import jax
import jax.numpy as jnp
from jax import lax
from jax.sharding import PartitionSpec as P


def silu_slope(values):
    sigma = jax.nn.sigmoid(values)
    return sigma * (1.0 + values * (1.0 - sigma))


def tile_products(tile_values, fetch_index, place_index, live_mask, source, out_tiles, forward):
    slots = tile_values.shape[0]
    tile_size = tile_values.shape[1]
    hidden = source.shape[-1]
    source_tiles = source.shape[0]
    source_flat = source.reshape(source_tiles, tile_size * hidden)
    group_size = math.gcd(slots, 64)
    turn_count = slots // group_size
    source_ids = jnp.arange(source_tiles, dtype=jnp.int32)
    out_ids = jnp.arange(out_tiles, dtype=jnp.int32)

    def step(running, step_index):
        offset = step_index * group_size
        blocks = lax.dynamic_slice_in_dim(tile_values, offset, group_size, 0)
        take = lax.dynamic_slice_in_dim(fetch_index, offset, group_size, 0)
        place = lax.dynamic_slice_in_dim(place_index, offset, group_size, 0)
        live_part = lax.dynamic_slice_in_dim(live_mask, offset, group_size, 0)
        take_onehot = (take[:, None] == source_ids[None, :]).astype(jnp.bfloat16)
        fetched = jnp.dot(take_onehot, source_flat, preferred_element_type=jnp.float32)
        fetched = fetched.astype(jnp.bfloat16).reshape(group_size, tile_size, hidden)
        if forward:
            product = jnp.einsum(
                "sab,sbf->saf", blocks, fetched, preferred_element_type=jnp.float32
            )
        else:
            product = jnp.einsum(
                "sab,saf->sbf", blocks, fetched, preferred_element_type=jnp.float32
            )
        place_onehot = (place[:, None] == out_ids[None, :]).astype(jnp.float32) * live_part[:, None]
        added = lax.dot_general(
            place_onehot,
            product.reshape(group_size, tile_size * hidden),
            (((0,), (0,)), ((), ())),
            precision=lax.Precision.HIGHEST,
            preferred_element_type=jnp.float32,
        )
        return (running + added, None)

    start_value = jnp.zeros((out_tiles, tile_size * hidden), jnp.float32)
    result = lax.scan(step, start_value, jnp.arange(turn_count, dtype=jnp.int32))[0]
    return result.reshape(out_tiles * tile_size, hidden)


def body(features, weight, tile_values, tile_row, tile_col, tile_count, cotangent):
    row_count = lax.axis_size("row")
    col_count = lax.axis_size("col")
    node_dev = features.shape[0]
    hidden = features.shape[1]
    tile_size = tile_values.shape[1]
    slots = tile_values.shape[0]
    row_tiles = node_dev * col_count // tile_size
    col_tiles = node_dev * row_count // tile_size
    live_mask = (jnp.arange(slots, dtype=jnp.int32) < tile_count[0, 0]).astype(jnp.float32)
    projected = jnp.dot(features, weight, preferred_element_type=jnp.float32).astype(jnp.bfloat16)
    panel_rows = lax.all_gather(projected, "row", axis=0, tiled=True).reshape(
        col_tiles, tile_size, hidden
    )
    forward_part = tile_products(
        tile_values, tile_col, tile_row, live_mask, panel_rows, row_tiles, True
    )
    forward_part = forward_part.astype(jnp.bfloat16)
    summed = lax.psum_scatter(forward_part, "col", scatter_dimension=0, tiled=True).astype(
        jnp.float32
    )
    activated = jax.nn.silu(summed).astype(jnp.bfloat16)
    slope = (cotangent.astype(jnp.float32) * silu_slope(summed)).astype(jnp.bfloat16)
    slope_full = lax.all_gather(slope, "col", axis=0, tiled=True)
    slope_tiles = slope_full.reshape(row_tiles, tile_size, hidden)
    column_part = tile_products(
        tile_values, tile_row, tile_col, live_mask, slope_tiles, col_tiles, False
    )
    column_part = column_part.astype(jnp.bfloat16)
    grad_nodes = (
        lax.psum_scatter(column_part, "row", scatter_dimension=0, tiled=True)
        .astype(jnp.float32)
        .astype(jnp.bfloat16)
    )
    grad_features = lax.dot_general(
        grad_nodes, weight, (((1,), (1,)), ((), ())), preferred_element_type=jnp.float32
    ).astype(jnp.bfloat16)
    weight_term = lax.dot_general(
        features, grad_nodes, (((0,), (0,)), ((), ())), preferred_element_type=jnp.float32
    )
    grad_weight = lax.psum(weight_term, ("row", "col"))
    return (activated, grad_features, grad_weight)


def solution(mesh):
    placed = (
        P(("col", "row"), None),
        P(),
        P(("row", "col"), None, None),
        P(("row", "col")),
        P(("row", "col")),
        P("row", "col"),
        P(("row", "col"), None),
    )
    return jax.shard_map(
        body,
        mesh=mesh,
        in_specs=placed,
        out_specs=(P(("row", "col"), None), P(("col", "row"), None), P()),
        check_vma=False,
    )
```

profile of v0, /device:TPU:0, one launch (start us, length us, event | category | flops | bytes accessed | tf_op | source)
XLA Modules:
  0.0 673.5 jit_solution(7849052803187527511)
XLA Ops:
  8.1 1.8 convolution_convert_fusion.3
  10.7 29.1 %all-gather.3.cloned.1.call-done = bf16[2048,256]{1,0:T(8,128)(2,1)} async-done(((bf16[512,256]{1,0:T(8,128)(2,1)}), bf16[2048,256]{1,0:T(8,128)(2,1)}) %all-gather.3.cloned.1.call-update) | async-done | bytes 1048592 | tf_op jit(solution)/shard_map/all_gather | solution.py:68
  41.4 196.9 %while.22 = (s32[]{:T(128)}, f32[32,32768]{1,0:T(8,128)}, s32[8]{0:T(128)S(1)}, s32[512]{0:T(512)}, f32[512]{0:T(512)S(1)}, /*index=5*/bf16[512,128,128]{2,1,0:T...) while((s32[]{:T(128)}, f32[32,32768]{1,0:T(8,128)}, ...), condition=%wide.region_1.2_spmd.clone, body=%wide.region_0.1_spmd.clone.sunk | while | flops 1413485568 | bytes 61868488 | solution.py:53
  45.8 2.9 fusion.64
  48.6 7.9 %copy.22 = f32[8,8,128,256]{3,1,2,0:T(8,128)} copy(f32[8,8,128,256]{3,2,1,0:T(8,128)S(1)} %bitcast.60) | data formatting | bytes 16777216 | tf_op jit(solution)/shard_map/while
  57.4 8.0 %convolution_add_fusion.4 = f32[32,32768]{1,0:T(8,128)} fusion(f32[64,32768]{1,0:T(8,128)} %bitcast.58, f32[32,32768]{1,0:T(8,128)} %get-tuple-element.327, pred[]{:T(512)S(6)} %compare.6, f32[64]{0:T(128)S(1)} %dynamic_slice.58, s32[64]{0:T(128)S(1)} %dynamic_slice.59), kind=kOutput, calls=%fused_computation.5.clone.1 | convolution fusion | flops 807407616 | bytes 16777728 | tf_op jit(solution)/shard_map/while/body/eval_jaxpr/dot_general | solution.py:43
  69.8 2.9 fusion.64
  72.7 7.9 %copy.22 = f32[8,8,128,256]{3,1,2,0:T(8,128)} copy(f32[8,8,128,256]{3,2,1,0:T(8,128)S(1)} %bitcast.60) | data formatting | bytes 16777216 | tf_op jit(solution)/shard_map/while
  81.4 8.7 %convolution_add_fusion.4 = f32[32,32768]{1,0:T(8,128)} fusion(f32[64,32768]{1,0:T(8,128)} %bitcast.58, f32[32,32768]{1,0:T(8,128)} %get-tuple-element.327, pred[]{:T(512)S(6)} %compare.6, f32[64]{0:T(128)S(1)} %dynamic_slice.58, s32[64]{0:T(128)S(1)} %dynamic_slice.59), kind=kOutput, calls=%fused_computation.5.clone.1 | convolution fusion | flops 807407616 | bytes 16777728 | tf_op jit(solution)/shard_map/while/body/eval_jaxpr/dot_general | solution.py:43
  94.5 2.9 fusion.64
  97.4 7.9 %copy.22 = f32[8,8,128,256]{3,1,2,0:T(8,128)} copy(f32[8,8,128,256]{3,2,1,0:T(8,128)S(1)} %bitcast.60) | data formatting | bytes 16777216 | tf_op jit(solution)/shard_map/while
  106.1 8.7 %convolution_add_fusion.4 = f32[32,32768]{1,0:T(8,128)} fusion(f32[64,32768]{1,0:T(8,128)} %bitcast.58, f32[32,32768]{1,0:T(8,128)} %get-tuple-element.327, pred[]{:T(512)S(6)} %compare.6, f32[64]{0:T(128)S(1)} %dynamic_slice.58, s32[64]{0:T(128)S(1)} %dynamic_slice.59), kind=kOutput, calls=%fused_computation.5.clone.1 | convolution fusion | flops 807407616 | bytes 16777728 | tf_op jit(solution)/shard_map/while/body/eval_jaxpr/dot_general | solution.py:43
  119.2 2.9 fusion.64
  122.0 7.9 %copy.22 = f32[8,8,128,256]{3,1,2,0:T(8,128)} copy(f32[8,8,128,256]{3,2,1,0:T(8,128)S(1)} %bitcast.60) | data formatting | bytes 16777216 | tf_op jit(solution)/shard_map/while
  130.8 8.7 %convolution_add_fusion.4 = f32[32,32768]{1,0:T(8,128)} fusion(f32[64,32768]{1,0:T(8,128)} %bitcast.58, f32[32,32768]{1,0:T(8,128)} %get-tuple-element.327, pred[]{:T(512)S(6)} %compare.6, f32[64]{0:T(128)S(1)} %dynamic_slice.58, s32[64]{0:T(128)S(1)} %dynamic_slice.59), kind=kOutput, calls=%fused_computation.5.clone.1 | convolution fusion | flops 807407616 | bytes 16777728 | tf_op jit(solution)/shard_map/while/body/eval_jaxpr/dot_general | solution.py:43
  143.9 2.9 fusion.64
  146.7 7.9 %copy.22 = f32[8,8,128,256]{3,1,2,0:T(8,128)} copy(f32[8,8,128,256]{3,2,1,0:T(8,128)S(1)} %bitcast.60) | data formatting | bytes 16777216 | tf_op jit(solution)/shard_map/while
  155.5 8.7 %convolution_add_fusion.4 = f32[32,32768]{1,0:T(8,128)} fusion(f32[64,32768]{1,0:T(8,128)} %bitcast.58, f32[32,32768]{1,0:T(8,128)} %get-tuple-element.327, pred[]{:T(512)S(6)} %compare.6, f32[64]{0:T(128)S(1)} %dynamic_slice.58, s32[64]{0:T(128)S(1)} %dynamic_slice.59), kind=kOutput, calls=%fused_computation.5.clone.1 | convolution fusion | flops 807407616 | bytes 16777728 | tf_op jit(solution)/shard_map/while/body/eval_jaxpr/dot_general | solution.py:43
  168.6 2.9 fusion.64
  171.4 7.9 %copy.22 = f32[8,8,128,256]{3,1,2,0:T(8,128)} copy(f32[8,8,128,256]{3,2,1,0:T(8,128)S(1)} %bitcast.60) | data formatting | bytes 16777216 | tf_op jit(solution)/shard_map/while
  180.2 8.7 %convolution_add_fusion.4 = f32[32,32768]{1,0:T(8,128)} fusion(f32[64,32768]{1,0:T(8,128)} %bitcast.58, f32[32,32768]{1,0:T(8,128)} %get-tuple-element.327, pred[]{:T(512)S(6)} %compare.6, f32[64]{0:T(128)S(1)} %dynamic_slice.58, s32[64]{0:T(128)S(1)} %dynamic_slice.59), kind=kOutput, calls=%fused_computation.5.clone.1 | convolution fusion | flops 807407616 | bytes 16777728 | tf_op jit(solution)/shard_map/while/body/eval_jaxpr/dot_general | solution.py:43
  193.3 2.9 fusion.64
  196.1 7.9 %copy.22 = f32[8,8,128,256]{3,1,2,0:T(8,128)} copy(f32[8,8,128,256]{3,2,1,0:T(8,128)S(1)} %bitcast.60) | data formatting | bytes 16777216 | tf_op jit(solution)/shard_map/while
  204.9 8.7 %convolution_add_fusion.4 = f32[32,32768]{1,0:T(8,128)} fusion(f32[64,32768]{1,0:T(8,128)} %bitcast.58, f32[32,32768]{1,0:T(8,128)} %get-tuple-element.327, pred[]{:T(512)S(6)} %compare.6, f32[64]{0:T(128)S(1)} %dynamic_slice.58, s32[64]{0:T(128)S(1)} %dynamic_slice.59), kind=kOutput, calls=%fused_computation.5.clone.1 | convolution fusion | flops 807407616 | bytes 16777728 | tf_op jit(solution)/shard_map/while/body/eval_jaxpr/dot_general | solution.py:43
  218.0 2.9 fusion.64
  220.8 7.9 %copy.22 = f32[8,8,128,256]{3,1,2,0:T(8,128)} copy(f32[8,8,128,256]{3,2,1,0:T(8,128)S(1)} %bitcast.60) | data formatting | bytes 16777216 | tf_op jit(solution)/shard_map/while
  229.6 8.7 %convolution_add_fusion.4 = f32[32,32768]{1,0:T(8,128)} fusion(f32[64,32768]{1,0:T(8,128)} %bitcast.58, f32[32,32768]{1,0:T(8,128)} %get-tuple-element.327, pred[]{:T(512)S(6)} %compare.6, f32[64]{0:T(128)S(1)} %dynamic_slice.58, s32[64]{0:T(128)S(1)} %dynamic_slice.59), kind=kOutput, calls=%fused_computation.5.clone.1 | convolution fusion | flops 807407616 | bytes 16777728 | tf_op jit(solution)/shard_map/while/body/eval_jaxpr/dot_general | solution.py:43
  238.3 2.4 convert_element_type.47
  240.7 2.4 convert_element_type.48
  243.3 35.7 %reduce-scatter.3.cloned.1.call-done = bf16[512,256]{1,0:T(8,128)(2,1)} async-done(((bf16[4096,256]{1,0:T(8,128)(2,1)}), bf16[512,256]{1,0:T(8,128)(2,1)}) %reduce-scatter.3.cloned.1.call-update) | async-done | bytes 262160 | tf_op jit(solution)/shard_map/reduce_scatter | solution.py:75
  279.0 2.0 fusion.33
  281.1 28.0 %all-gather.5.cloned.1.call-done = bf16[4096,256]{1,0:T(8,128)(2,1)} async-done(((bf16[512,256]{1,0:T(8,128)(2,1)}), bf16[4096,256]{1,0:T(8,128)(2,1)}) %all-gather.5.cloned.1.call-update) | async-done | bytes 2097168 | tf_op jit(solution)/shard_map/all_gather | solution.py:80
  309.1 2.9 reshape_reshape.7
  311.9 190.9 %while.23 = (s32[]{:T(128)}, f32[16,32768]{1,0:T(8,128)}, s32[8]{0:T(128)S(1)}, s32[512]{0:T(512)}, f32[512]{0:T(512)S(1)}, /*index=5*/bf16[512,128,128]{2,1,0:T...) while((s32[]{:T(128)}, f32[16,32768]{1,0:T(8,128)}, ...), condition=%wide.region_4.5_spmd.clone, body=%wide.region_3.4_spmd.clone.sunk | while | flops 1076891648 | bytes 58722760 | solution.py:53
  316.4 2.9 fusion.70
  319.3 7.9 %copy.24 = f32[8,8,128,256]{3,1,2,0:T(8,128)} copy(f32[8,8,128,256]{3,2,1,0:T(8,128)S(1)} %bitcast.61) | data formatting | bytes 16777216 | tf_op jit(solution)/shard_map/while
  328.1 7.5 %convolution_add_fusion.5 = f32[16,32768]{1,0:T(8,128)} fusion(f32[64,32768]{1,0:T(8,128)} %bitcast.59, f32[16,32768]{1,0:T(8,128)} %get-tuple-element.363, pred[]{:T(512)S(6)} %compare.7, f32[64]{0:T(128)S(1)} %dynamic_slice.63, s32[64]{0:T(128)S(1)} %dynamic_slice.64), kind=kOutput, calls=%fused_computation.18.clone.1 | convolution fusion | flops 403703808 | bytes 12583425 | tf_op jit(solution)/shard_map/while/body/eval_jaxpr/dot_general | solution.py:43
  340.0 2.9 fusion.70
  342.9 7.9 %copy.24 = f32[8,8,128,256]{3,1,2,0:T(8,128)} copy(f32[8,8,128,256]{3,2,1,0:T(8,128)S(1)} %bitcast.61) | data formatting | bytes 16777216 | tf_op jit(solution)/shard_map/while
  351.7 7.8 %convolution_add_fusion.5 = f32[16,32768]{1,0:T(8,128)} fusion(f32[64,32768]{1,0:T(8,128)} %bitcast.59, f32[16,32768]{1,0:T(8,128)} %get-tuple-element.363, pred[]{:T(512)S(6)} %compare.7, f32[64]{0:T(128)S(1)} %dynamic_slice.63, s32[64]{0:T(128)S(1)} %dynamic_slice.64), kind=kOutput, calls=%fused_computation.18.clone.1 | convolution fusion | flops 403703808 | bytes 12583425 | tf_op jit(solution)/shard_map/while/body/eval_jaxpr/dot_general | solution.py:43
  363.9 2.9 fusion.70
  366.8 7.9 %copy.24 = f32[8,8,128,256]{3,1,2,0:T(8,128)} copy(f32[8,8,128,256]{3,2,1,0:T(8,128)S(1)} %bitcast.61) | data formatting | bytes 16777216 | tf_op jit(solution)/shard_map/while
  375.6 7.8 %convolution_add_fusion.5 = f32[16,32768]{1,0:T(8,128)} fusion(f32[64,32768]{1,0:T(8,128)} %bitcast.59, f32[16,32768]{1,0:T(8,128)} %get-tuple-element.363, pred[]{:T(512)S(6)} %compare.7, f32[64]{0:T(128)S(1)} %dynamic_slice.63, s32[64]{0:T(128)S(1)} %dynamic_slice.64), kind=kOutput, calls=%fused_computation.18.clone.1 | convolution fusion | flops 403703808 | bytes 12583425 | tf_op jit(solution)/shard_map/while/body/eval_jaxpr/dot_general | solution.py:43
  387.8 2.9 fusion.70
  390.7 7.9 %copy.24 = f32[8,8,128,256]{3,1,2,0:T(8,128)} copy(f32[8,8,128,256]{3,2,1,0:T(8,128)S(1)} %bitcast.61) | data formatting | bytes 16777216 | tf_op jit(solution)/shard_map/while
  399.5 7.8 %convolution_add_fusion.5 = f32[16,32768]{1,0:T(8,128)} fusion(f32[64,32768]{1,0:T(8,128)} %bitcast.59, f32[16,32768]{1,0:T(8,128)} %get-tuple-element.363, pred[]{:T(512)S(6)} %compare.7, f32[64]{0:T(128)S(1)} %dynamic_slice.63, s32[64]{0:T(128)S(1)} %dynamic_slice.64), kind=kOutput, calls=%fused_computation.18.clone.1 | convolution fusion | flops 403703808 | bytes 12583425 | tf_op jit(solution)/shard_map/while/body/eval_jaxpr/dot_general | solution.py:43
  411.7 2.9 fusion.70
  414.6 7.9 %copy.24 = f32[8,8,128,256]{3,1,2,0:T(8,128)} copy(f32[8,8,128,256]{3,2,1,0:T(8,128)S(1)} %bitcast.61) | data formatting | bytes 16777216 | tf_op jit(solution)/shard_map/while
  423.4 7.8 %convolution_add_fusion.5 = f32[16,32768]{1,0:T(8,128)} fusion(f32[64,32768]{1,0:T(8,128)} %bitcast.59, f32[16,32768]{1,0:T(8,128)} %get-tuple-element.363, pred[]{:T(512)S(6)} %compare.7, f32[64]{0:T(128)S(1)} %dynamic_slice.63, s32[64]{0:T(128)S(1)} %dynamic_slice.64), kind=kOutput, calls=%fused_computation.18.clone.1 | convolution fusion | flops 403703808 | bytes 12583425 | tf_op jit(solution)/shard_map/while/body/eval_jaxpr/dot_general | solution.py:43
  435.6 2.9 fusion.70
  438.5 7.9 %copy.24 = f32[8,8,128,256]{3,1,2,0:T(8,128)} copy(f32[8,8,128,256]{3,2,1,0:T(8,128)S(1)} %bitcast.61) | data formatting | bytes 16777216 | tf_op jit(solution)/shard_map/while
  447.3 7.8 %convolution_add_fusion.5 = f32[16,32768]{1,0:T(8,128)} fusion(f32[64,32768]{1,0:T(8,128)} %bitcast.59, f32[16,32768]{1,0:T(8,128)} %get-tuple-element.363, pred[]{:T(512)S(6)} %compare.7, f32[64]{0:T(128)S(1)} %dynamic_slice.63, s32[64]{0:T(128)S(1)} %dynamic_slice.64), kind=kOutput, calls=%fused_computation.18.clone.1 | convolution fusion | flops 403703808 | bytes 12583425 | tf_op jit(solution)/shard_map/while/body/eval_jaxpr/dot_general | solution.py:43
  459.5 2.9 fusion.70
  462.4 7.9 %copy.24 = f32[8,8,128,256]{3,1,2,0:T(8,128)} copy(f32[8,8,128,256]{3,2,1,0:T(8,128)S(1)} %bitcast.61) | data formatting | bytes 16777216 | tf_op jit(solution)/shard_map/while
  471.1 7.8 %convolution_add_fusion.5 = f32[16,32768]{1,0:T(8,128)} fusion(f32[64,32768]{1,0:T(8,128)} %bitcast.59, f32[16,32768]{1,0:T(8,128)} %get-tuple-element.363, pred[]{:T(512)S(6)} %compare.7, f32[64]{0:T(128)S(1)} %dynamic_slice.63, s32[64]{0:T(128)S(1)} %dynamic_slice.64), kind=kOutput, calls=%fused_computation.18.clone.1 | convolution fusion | flops 403703808 | bytes 12583425 | tf_op jit(solution)/shard_map/while/body/eval_jaxpr/dot_general | solution.py:43
  483.4 2.9 fusion.70
  486.3 7.9 %copy.24 = f32[8,8,128,256]{3,1,2,0:T(8,128)} copy(f32[8,8,128,256]{3,2,1,0:T(8,128)S(1)} %bitcast.61) | data formatting | bytes 16777216 | tf_op jit(solution)/shard_map/while
  495.0 7.8 %convolution_add_fusion.5 = f32[16,32768]{1,0:T(8,128)} fusion(f32[64,32768]{1,0:T(8,128)} %bitcast.59, f32[16,32768]{1,0:T(8,128)} %get-tuple-element.363, pred[]{:T(512)S(6)} %compare.7, f32[64]{0:T(128)S(1)} %dynamic_slice.63, s32[64]{0:T(128)S(1)} %dynamic_slice.64), kind=kOutput, calls=%fused_computation.18.clone.1 | convolution fusion | flops 403703808 | bytes 12583425 | tf_op jit(solution)/shard_map/while/body/eval_jaxpr/dot_general | solution.py:43
  502.9 1.7 convert_element_type.53
  506.0 27.4 %reduce-scatter.5.cloned.1.call-done = bf16[512,256]{1,0:T(8,128)(2,1)} async-done(((bf16[2048,256]{1,0:T(8,128)(2,1)}), bf16[512,256]{1,0:T(8,128)(2,1)}) %reduce-scatter.5.cloned.1.call-update) | async-done | bytes 262160 | tf_op jit(solution)/shard_map/reduce_scatter | solution.py:87
  533.4 1.9 convolution_bitcast_fusion
  535.3 1.9 convolution_convert_fusion.2
  537.2 128.0 %all-reduce.2.cloned.1.call-done = f32[256,256]{0,1:T(8,128)} async-done(((f32[256,256]{0,1:T(8,128)}), f32[256,256]{0,1:T(8,128)}) %all-reduce.2.cloned.1.call-update) | async-done | bytes 262160 | tf_op jit(solution)/shard_map/psum | solution.py:97
  665.2 1.8 copy.11
  (119 shorter events, 77.1 us)
Async XLA Ops:
  7.2 1.0 copy-start
  7.2 32.6 %all-gather.3.cloned.1.call-start = ((), (), s32[]{:S(2)}) async-start(), calls=%async_computation.2 | async-start | bytes 1310720 | tf_op jit(solution)/shard_map/all_gather | solution.py:68
  10.0 269.0 %reduce-scatter.3.cloned.1.call-start = ((), (), s32[]{:S(2)}) async-start(), calls=%async_computation.3 | async-start | bytes 2359296 | tf_op jit(solution)/shard_map/reduce_scatter | solution.py:75
  240.7 38.3 %copy-start.2 = (bf16[512,256]{1,0:T(8,128)(2,1)S(1)}, bf16[512,256]{1,0:T(8,128)(2,1)}, u32[]{:S(2)}) copy-start(bf16[512,256]{1,0:T(8,128)(2,1)} %param.17) | copy-start | bytes 786436
  243.1 66.0 %all-gather.5.cloned.1.call-start = ((), (), s32[]{:S(2)}) async-start(), calls=%async_computation.4 | async-start | bytes 2359296 | tf_op jit(solution)/shard_map/all_gather | solution.py:80
  281.0 252.3 %reduce-scatter.5.cloned.1.call-start = ((), (), s32[]{:S(2)}) async-start(), calls=%async_computation.5 | async-start | bytes 1310720 | tf_op jit(solution)/shard_map/reduce_scatter | solution.py:87
  502.9 32.4 %copy-start.1 = (bf16[256,256]{1,0:T(8,128)(2,1)S(1)}, bf16[256,256]{1,0:T(8,128)(2,1)}, u32[]{:S(2)}) copy-start(bf16[256,256]{1,0:T(8,128)(2,1)} %param.12) | copy-start | bytes 393220
  505.9 159.3 %all-reduce.2.cloned.1.call-start = ((), (), s32[]{:S(2)}) async-start(), calls=%async_computation.6 | async-start | bytes 524288 | tf_op jit(solution)/shard_map/psum | solution.py:97
Sparse Core Ops, SparseCore 0:
  10.4 29.3 all-gather.2
  243.2 35.7 reduce-scatter.2
  281.2 27.8 all-gather.4
  506.0 27.2 reduce-scatter.4
  540.2 124.9 all-reduce.1
where the time goes:
time: 675 us; the launch traced here: 674 us
  waiting for transfers between devices  248 us (37%)
  matrix products  203 us (30%)
  local copies, waits for them, and re-layouts  190 us (28%)
  between operations  14.5 us (2%)
  loops' own time  10.9 us (2%)
    while x32, local copies, waits for them, and re-layouts  145 us
    dot_general x16, matrix products, step(): lax.dot_general(place_onehot, product.reshape(group_size, tile_size * hid...  131 us
    psum x1, waiting for transfers between devices, body(): grad_weight = lax.psum(weight_term, ('row', 'col'))  128 us
    reduce_scatter x1, waiting for transfers between devices, body(): lax.psum_scatter(forward_part, 'col', scatter_dimension=0, tiled=True)  35.7 us
    all_gather x1, waiting for transfers between devices, body(): lax.all_gather(projected, 'row', axis=0, tiled=True)  29.1 us
    all_gather x1, waiting for transfers between devices, body(): slope_full = lax.all_gather(slope, 'col', axis=0, tiled=True)  28 us
    reduce_scatter x1, waiting for transfers between devices, body(): lax.psum_scatter(column_part, 'row', scatter_dimension=0, tiled=True)  27.4 us
    dot_general x8, matrix products, step(): jnp.einsum('sab,saf->sbf', blocks, fetched, preferred_element_type=jnp.fl...  23.3 us
  transfers between devices with their start and end apart: 5, of which 5 were waited for; matrix products, arithmetic and copies ran while one was open for 0% of the time, Pallas kernels for 0%

commit v1 on v0

--- a/solution.py
+++ b/solution.py
@@ -1,9 +1,19 @@
+import functools
 import math
 
 import jax
 import jax.numpy as jnp
 from jax import lax
+from jax.experimental import pallas as pl
+from jax.experimental.pallas import tpu as pltpu
 from jax.sharding import PartitionSpec as P
+
+F32 = jnp.float32
+BF16 = jnp.bfloat16
+IN_VMEM = pl.BlockSpec(memory_space=pltpu.VMEM)
+IN_SMEM = pl.BlockSpec(memory_space=pltpu.SMEM)
+IN_PLACE = pl.BlockSpec(memory_space=pl.ANY)
+VMEM_LIMIT = 12 * 2**20
 
 
 def silu_slope(values):
@@ -54,7 +64,7 @@
     return result.reshape(out_tiles * tile_size, hidden)
 
 
-def body(features, weight, tile_values, tile_row, tile_col, tile_count, cotangent):
+def sparse_body(features, weight, tile_values, tile_row, tile_col, tile_count, cotangent):
     row_count = lax.axis_size("row")
     col_count = lax.axis_size("col")
     node_dev = features.shape[0]
@@ -98,6 +108,254 @@
     return (activated, grad_features, grad_weight)
 
 
+def kernel_call(kernel, out_shape, arguments, name, flops=0, scratch=(), in_specs=None, after=()):
+    count = len(arguments)
+
+    def ordered(*refs):
+        kernel(*refs[:count], *refs[count + len(after) :])
+
+    return pl.pallas_call(
+        ordered if after else kernel,
+        out_shape=out_shape,
+        in_specs=(in_specs or [IN_VMEM] * count) + [IN_PLACE] * len(after),
+        out_specs=jax.tree.map(lambda _: IN_VMEM, out_shape),
+        scratch_shapes=list(scratch),
+        compiler_params=pltpu.CompilerParams(vmem_limit_bytes=VMEM_LIMIT),
+        cost_estimate=pl.CostEstimate(flops=flops, bytes_accessed=0, transcendentals=0),
+        name=name,
+    )(*arguments, *after)
+
+
+def later(values, after):
+    return pl.pallas_call(
+        lambda *refs: None,
+        out_shape=[jax.ShapeDtypeStruct(value.shape, value.dtype) for value in values],
+        in_specs=[IN_PLACE] * (len(values) + len(after)),
+        out_specs=[IN_PLACE] * len(values),
+        input_output_aliases={i: i for i in range(len(values))},
+        compiler_params=pltpu.CompilerParams(vmem_limit_bytes=VMEM_LIMIT),
+        name="later",
+    )(*values, *after)
+
+
+def held(value):
+    return pltpu.with_memory_space_constraint(value, pltpu.VMEM)
+
+
+def swap(value, axis, distance):
+    count = lax.axis_size(axis)
+    return lax.ppermute(value, axis, [(i, i ^ distance) for i in range(count)])
+
+
+def load_kernel(count_ref, row_ref, col_ref, tiles_ref, adjacency_ref, rows_ref, cols_ref, zero_ref, sem, sems):
+    slots, tile, _ = tiles_ref.shape
+    row_copy = pltpu.make_async_copy(row_ref, rows_ref, sems.at[0])
+    col_copy = pltpu.make_async_copy(col_ref, cols_ref, sems.at[1])
+    row_copy.start()
+    col_copy.start()
+    row_flip = lax.axis_index("col") * (adjacency_ref.shape[0] // lax.axis_size("col") // tile)
+    col_flip = lax.axis_index("row") * (adjacency_ref.shape[1] // lax.axis_size("row") // tile)
+    zero_ref[...] = jnp.zeros_like(zero_ref)
+    row_copy.wait()
+    col_copy.wait()
+
+    def target(slot):
+        top = pl.multiple_of((rows_ref[slot] ^ row_flip) * tile, tile)
+        left = pl.multiple_of((cols_ref[slot] ^ col_flip) * tile, tile)
+        return adjacency_ref.at[pl.ds(top, tile), pl.ds(left, tile)]
+
+    def live(slot, carry):
+        pltpu.make_async_copy(tiles_ref.at[slot], target(slot), sem).start()
+        return carry
+
+    def dead(slot, carry):
+        pltpu.make_async_copy(zero_ref, target(slot), sem).start()
+        return carry
+
+    count = count_ref[0, 0]
+    lax.fori_loop(0, count, live, 0)
+    lax.fori_loop(count, slots, dead, 0)
+    pltpu.make_async_copy(adjacency_ref, adjacency_ref, sem).wait()
+
+
+def forward_kernel(slots, adjacency_ref, *refs):
+    source = jnp.concatenate([ref[...] for ref in refs[:4]], axis=0)
+    others, out_refs = refs[4 : -len(slots)], refs[-len(slots) :]
+    nodes = refs[0].shape[0]
+    for i, slot in enumerate(slots):
+        total = jnp.dot(adjacency_ref[nodes * slot : nodes * (slot + 1), :], source, preferred_element_type=F32)
+        if others:
+            total = total + others[i][...].astype(F32)
+        out_refs[i][...] = total.astype(out_refs[i].dtype)
+
+
+def add_kernel(*refs):
+    count = len(refs) // 3
+    for mine, other, out in zip(refs[:count], refs[count : 2 * count], refs[2 * count :]):
+        out[...] = (mine[...] + other[...].astype(F32)).astype(out.dtype)
+
+
+def middle_kernel(weight_ref, cotangent_ref, mine_ref, r1_ref, r2_ref, r3_ref,
+                  activated_ref, sent_ref, keep_ref, send_ref, term_ref):
+    mixed = mine_ref[...] + r1_ref[...].astype(F32) + r2_ref[...].astype(F32) + r3_ref[...].astype(F32)
+    mixed = mixed.astype(BF16)
+    weight = weight_ref[...]
+    summed = jnp.dot(mixed, weight, preferred_element_type=F32)
+    sigma = 1.0 / (1.0 + jnp.exp(-summed))
+    activated_ref[...] = (summed * sigma).astype(BF16)
+    slope = cotangent_ref[...].astype(F32) * sigma * (1.0 + summed * (1.0 - sigma))
+    slope = slope.astype(BF16)
+    sent_ref[...] = lax.dot_general(
+        slope, weight, (((1,), (1,)), ((), ())), preferred_element_type=F32
+    ).astype(BF16)
+    term_ref[...] = lax.dot_general(mixed, slope, (((0,), (0,)), ((), ())), preferred_element_type=F32)
+    half = keep_ref.shape[0]
+    core = lax.axis_index("col") % 2
+    keep_ref[...] = term_ref[pl.ds(pl.multiple_of(core * half, half), half), :]
+    send_ref[...] = term_ref[pl.ds(pl.multiple_of((1 - core) * half, half), half), :]
+
+
+def backward_block(slots, chunk, nodes, adjacency_ref, source):
+    left = nodes * chunk
+    block = jnp.concatenate(
+        [adjacency_ref[nodes * slot : nodes * (slot + 1), left : left + nodes] for slot in slots], axis=0
+    )
+    return lax.dot_general(block, source, (((0,), (0,)), ((), ())), preferred_element_type=F32)
+
+
+def backward_near_kernel(slots, adjacency_ref, *refs):
+    source = jnp.concatenate([ref[...] for ref in refs[: len(slots)]], axis=0)
+    out_ref = refs[-1]
+    nodes = refs[0].shape[0]
+    for chunk in range(out_ref.shape[0] // nodes):
+        out_ref[nodes * chunk : nodes * (chunk + 1), :] = backward_block(slots, chunk, nodes, adjacency_ref, source)
+
+
+def backward_home_kernel(slots, adjacency_ref, start_ref, *refs):
+    source = jnp.concatenate([ref[...] for ref in refs[: len(slots)]], axis=0)
+    out_ref = refs[-1]
+    nodes = refs[0].shape[0]
+    for chunk in range(out_ref.shape[0] // nodes):
+        here = slice(nodes * chunk, nodes * (chunk + 1))
+        out_ref[here, :] = start_ref[here, :] + backward_block(slots, chunk, nodes, adjacency_ref, source)
+
+
+def backward_away_kernel(slots, chunks, adjacency_ref, start_ref, *refs):
+    source = jnp.concatenate([ref[...] for ref in refs[: len(slots)]], axis=0)
+    nodes = refs[0].shape[0]
+    for out_ref, chunk in zip(refs[len(slots) :], chunks):
+        here = slice(nodes * chunk, nodes * (chunk + 1))
+        total = start_ref[here, :] + backward_block(slots, chunk, nodes, adjacency_ref, source)
+        out_ref[...] = total.astype(out_ref.dtype)
+
+
+def finish_kernel(mine_ref, q1_ref, q2_ref, q3_ref, half_ref, other_ref, nodes_ref, weight_ref):
+    total = mine_ref[...] + q1_ref[...].astype(F32) + q2_ref[...].astype(F32) + q3_ref[...].astype(F32)
+    nodes_ref[...] = total.astype(nodes_ref.dtype)
+    half = half_ref.shape[0]
+    core = lax.axis_index("col") % 2
+    weight_ref[pl.ds(pl.multiple_of(core * half, half), half), :] = half_ref[...]
+    weight_ref[pl.ds(pl.multiple_of((1 - core) * half, half), half), :] = other_ref[...]
+
+
+def sum_kernel(mine_ref, other_ref, out_ref):
+    out_ref[...] = mine_ref[...] + other_ref[...]
+
+
+def dense_body(features, weight, tile_values, tile_row, tile_col, tile_count, cotangent):
+    nodes, hidden = features.shape
+    slots, tile = tile_values.shape[:2]
+    rows, cols = nodes * lax.axis_size("col"), nodes * lax.axis_size("row")
+    block = jax.ShapeDtypeStruct((nodes, hidden), BF16)
+    exact = pltpu.VMEM((nodes, hidden), F32)
+    running = pltpu.VMEM((cols, hidden), F32)
+    whole, half = (jax.ShapeDtypeStruct((hidden // n, hidden), F32) for n in (1, 2))
+    slot_flops = 2 * nodes * cols * hidden
+
+    def in_hbm(value):
+        return pltpu.with_memory_space_constraint(value, pltpu.HBM)
+
+    adjacency = kernel_call(
+        load_kernel,
+        pltpu.VMEM((rows, cols), BF16),
+        (tile_count, in_hbm(tile_row), in_hbm(tile_col), in_hbm(tile_values)),
+        "load_tiles",
+        scratch=(
+            pltpu.SMEM((slots,), jnp.int32),
+            pltpu.SMEM((slots,), jnp.int32),
+            pltpu.VMEM((tile, tile), BF16),
+            pltpu.SemaphoreType.DMA,
+            pltpu.SemaphoreType.DMA((2,)),
+        ),
+        in_specs=[IN_SMEM, IN_PLACE, IN_PLACE, IN_PLACE],
+    )
+    adjacency = held(adjacency)
+    source = [features] + [swap(features, "row", d) for d in (1, 2, 3)]
+
+    def forward(slot_ids, kind, name, others=(), after=()):
+        return kernel_call(
+            functools.partial(forward_kernel, slot_ids), [kind] * len(slot_ids) if not isinstance(kind, list) else kind,
+            (adjacency, *source, *others), name, flops=slot_flops * len(slot_ids), after=after,
+        )
+
+    away_far = [swap(value, "col", 1) for value in forward((7, 5), block, "forward_away_far")]
+    home_far = [held(value) for value in forward((6, 4), exact, "forward_home_far")]
+    far = kernel_call(add_kernel, [block] * 2, (*home_far, *away_far), "add_far")
+    away_near = forward((3, 1), block, "forward_away_near", after=(far[0],))
+    away_near = [swap(value, "col", 1) for value in away_near]
+    r3, r2 = swap(far[0], "col", 6), swap(far[1], "col", 4)
+    near, mine = forward((2, 0), [block, exact], "forward_home_near", others=away_near)
+    r1 = swap(near, "col", 2)
+    activated, sent, keep, send = kernel_call(
+        middle_kernel, [block, block, half, half], (weight, cotangent, held(mine), r1, r2, r3), "middle",
+        scratch=(pltpu.VMEM(whole.shape, F32),),
+    )
+
+    s3, s2, s1 = (swap(sent, "col", 2 * d) for d in (3, 2, 1))
+    o0, o1 = swap(sent, "col", 1), swap(s1, "col", 1)
+
+    def add(value, axis, distance, after=()):
+        return kernel_call(sum_kernel, half, (value, swap(value, axis, distance)), "weight_sum", after=after)
+
+    term = kernel_call(sum_kernel, half, (keep, swap(send, "col", 1)), "weight_sum")
+    term = add(term, "row", 1)
+    term = add(term, "row", 2)
+    start = kernel_call(
+        functools.partial(backward_near_kernel, (0, 2)), running, (adjacency, sent, s1),
+        "backward_home", flops=2 * slot_flops,
+    )
+    s2, s3 = later((s2, s3), (start, term))
+    o2, o3 = swap(s2, "col", 1), swap(s3, "col", 1)
+    start = kernel_call(
+        functools.partial(backward_home_kernel, (1, 3, 4, 6)), running, (adjacency, held(start), o0, o1, s2, s3),
+        "backward_most", flops=4 * slot_flops,
+    )
+    shares = kernel_call(
+        functools.partial(backward_away_kernel, (5, 7), (3, 2, 1)), [block] * 3,
+        (adjacency, held(start), o2, o3), "backward_far_away", flops=3 * slot_flops // 2,
+    )
+    returned = [swap(share, "row", d) for share, d in zip(shares, (3, 2, 1))]
+    mine = kernel_call(
+        functools.partial(backward_away_kernel, (5, 7), (0,)), [exact],
+        (adjacency, held(start), o2, o3), "backward_mine", flops=slot_flops // 2, after=(shares[0],),
+    )[0]
+    term = add(term, "col", 2, after=(mine,))
+    term = add(term, "col", 4)
+    grad_features, grad_weight = kernel_call(
+        finish_kernel, [block, whole], (held(mine), *returned, term, swap(term, "col", 1)), "finish"
+    )
+    return (activated, grad_features, grad_weight)
+
+
+def body(*arguments):
+    features, tile_values = arguments[0], arguments[2]
+    row_count, col_count = lax.axis_size("row"), lax.axis_size("col")
+    cells = (features.shape[0] // tile_values.shape[1]) ** 2 * row_count * col_count
+    if cells == tile_values.shape[0] and (row_count, col_count) == (4, 8):
+        return dense_body(*arguments)
+    return sparse_body(*arguments)
+
+
 def solution(mesh):
     placed = (
         P(("col", "row"), None),

time: 675 us -> 98.9 us (0.15)
  matrix products: 203 us -> 0 us
  waiting for transfers between devices: 248 us -> 49.8 us
  local copies, waits for them, and re-layouts: 190 us -> 0.02 us
  starting transfers between devices: 0.39 us -> 28.3 us
  Pallas kernels: 0 us -> 19.1 us
  between operations: 14.5 us -> 1.49 us
  loops' own time: 10.9 us -> 0 us
    dot_general x51 -> x0, matrix products: 203 us -> none  [the longest x16 131 us: step(): lax.dot_general(place_onehot, product.reshape(group_size, tile_size * hid...]
    while x32 -> x0, local copies, waits for them, and re-layouts: 145 us -> none
    psum x1 -> x0, waiting for transfers between devices: 128 us -> none  [body(): grad_weight = lax.psum(weight_term, ('row', 'col'))]
    reduce_scatter x2 -> x0, waiting for transfers between devices: 63.1 us -> none  [the longest x1 35.7 us: body(): lax.psum_scatter(forward_part, 'col', scatter_dimension=0, tiled=True)]
    all_gather x2 -> x0, waiting for transfers between devices: 57.1 us -> none  [the longest x1 29.1 us: body(): lax.all_gather(projected, 'row', axis=0, tiled=True)]
    ppermute x0 -> x26, waiting for transfers between devices: none -> 49.8 us  [swap(): return lax.ppermute(value, axis, [(i, i ^ distance) for i in range(count)])]
    dynamic_slice x64 -> x0, local copies, waits for them, and re-layouts: 34.7 us -> none  [the longest x16 12.1 us: step(): take = lax.dynamic_slice_in_dim(fetch_index, offset, group_size, 0)]
    ppermute x0 -> x26, starting transfers between devices: none -> 28.3 us  [swap(): return lax.ppermute(value, axis, [(i, i ^ distance) for i in range(count)])]
  transfers between devices with their start and end apart: 5 -> 26, of which waited for: 5 -> 9; matrix products, arithmetic and copies ran while one was open for 0% -> 0% of each run, Pallas kernels for 0% -> 15%
where the time goes in v1:
time: 98.9 us; the launch traced here: 98.7 us
  waiting for transfers between devices  49.8 us (50%)
  starting transfers between devices  28.3 us (29%)
  Pallas kernels  19.1 us (19%)
  between operations  1.49 us (2%)
    ppermute x26, waiting for transfers between devices, swap(): return lax.ppermute(value, axis, [(i, i ^ distance) for i in range(count)])  49.8 us
    ppermute x26, starting transfers between devices, swap(): return lax.ppermute(value, axis, [(i, i ^ distance) for i in range(count)])  28.3 us
    pallas_call x17, Pallas kernels, kernel_call(): pl.pallas_call(ordered if after else kernel, out_shape=out_shape, in_spec...  19.1 us
  transfers between devices with their start and end apart: 26, of which 9 were waited for; matrix products, arithmetic and copies ran while one was open for 0% of the time, Pallas kernels for 15%

profile of v1, /device:TPU:0, one launch (start us, length us, event | category | flops | bytes accessed | tf_op | source)
XLA Modules:
  0.0 98.7 jit_solution(5332613548572378573)
XLA Ops:
  0.6 3.0 %collective-permute-start = (bf16[512,256]{1,0:T(8,128)(2,1)}, bf16[512,256]{1,0:T(8,128)(2,1)S(1)}, u32[]{:S(2)}, u32[]{:S(2)}) collective-permute-start(bf16[512,256]{1,0:T(8,128)(2,1)} %refs_0_.5), channel_id=1, source_target_pairs={{0,8},{8,0},{16,24},{24,16},{1,9},{9,1},{17,25},{25,17},{2,10},{10... | collective-permute-start | bytes 786440 | tf_op jit(solution)/shard_map/ppermute | solution.py:147
  3.6 1.5 %collective-permute-start.1 = (bf16[512,256]{1,0:T(8,128)(2,1)}, bf16[512,256]{1,0:T(8,128)(2,1)S(1)}, u32[]{:S(2)}, u32[]{:S(2)}) collective-permute-start(bf16[512,256]{1,0:T(8,128)(2,1)} %refs_0_.5), channel_id=1, source_target_pairs={{0,16},{8,24},{16,0},{24,8},{1,17},{9,25},{17,1},{25,9},{2,18},{10... | collective-permute-start | bytes 786440 | tf_op jit(solution)/shard_map/ppermute | solution.py:147
  5.2 0.0 collective-permute-start.2
  5.8 6.6 %load_tiles.1.adjacency_ref.refs_0_ = bf16[4096,2048]{1,0:T(8,128)(2,1)S(1)} custom-call(s32[1,1]{1,0:T(1,128)S(6)} %copy.14.count_ref, s32[512]{0:T(512)} %row_ref.1, s32[512]{0:T(512)} %col_ref.1, bf16[512,128,128]{2,1,0:T(8,128)(2,1)} %tiles_ref.1), custom_call_target="tpu_custom_call" | custom-call | tf_op jit(solution)/shard_map/load_tiles/pallas_call | solution.py:117
  12.4 0.0 collective-permute-done.refs_1_.refs_2_
  12.4 4.8 %collective-permute-done.1.refs_2_.refs_3_ = bf16[512,256]{1,0:T(8,128)(2,1)S(1)} collective-permute-done((bf16[512,256]{1,0:T(8,128)(2,1)}, bf16[512,256]{1,0:T(8,128)(2,1)S(1)}, u32[]{:S(2)}, u32[]{:S(2)}) %collective-permute-start.1) | collective-permute-done | bytes 262176 | tf_op jit(solution)/shard_map/ppermute | solution.py:147
  17.2 0.0 collective-permute-done.2.refs_3_.refs_4_
  17.2 1.3 %forward_away_far.1 = (bf16[512,256]{1,0:T(8,128)(2,1)S(1)}, bf16[512,256]{1,0:T(8,128)(2,1)S(1)}) custom-call(bf16[4096,2048]{1,0:T(8,128)(2,1)S(1)} %load_tiles.1.adjacency_ref.refs_0_, bf16[512,256]{1,0:T(8,128)(2,1)S(1)} %copy-done, bf16[512,256]{1,0:T(8,128)(2,1)S(1)} %collective-permute-done.refs_1_.refs_2_, ...), custom_call_target="tpu_custom_call" | custom-call | flops 1073741824 | tf_op jit(solution)/shard_map/forward_away_far/pallas_call | solution.py:117
  18.5 0.1 collective-permute-start.3
  18.6 0.5 collective-permute-start.4
  19.1 1.2 %forward_home_far.1 = (f32[512,256]{1,0:T(8,128)S(1)}, f32[512,256]{1,0:T(8,128)S(1)}) custom-call(bf16[4096,2048]{1,0:T(8,128)(2,1)S(1)} %load_tiles.1.adjacency_ref.refs_0_, bf16[512,256]{1,0:T(8,128)(2,1)S(1)} %copy-done, bf16[512,256]{1,0:T(8,128)(2,1)S(1)} %collective-permute-done.refs_1_.refs_2_, ...), custom_call_target="tpu_custom_call" | custom-call | flops 1073741824 | tf_op jit(solution)/shard_map/forward_home_far/pallas_call | solution.py:117
  20.3 0.0 collective-permute-done.3.refs_2_
  20.3 0.1 collective-permute-done.4.refs_3_
  20.5 0.1 add_far.1
  20.6 0.0 copy-start.1
  20.6 0.0 copy-start.2
  20.6 1.3 %forward_away_near.1 = (bf16[512,256]{1,0:T(8,128)(2,1)S(1)}, bf16[512,256]{1,0:T(8,128)(2,1)S(1)}) custom-call(bf16[4096,2048]{1,0:T(8,128)(2,1)S(1)} %load_tiles.1.adjacency_ref.refs_0_, bf16[512,256]{1,0:T(8,128)(2,1)S(1)} %copy-done, bf16[512,256]{1,0:T(8,128)(2,1)S(1)} %collective-permute-done.refs_1_.refs_2_, ...), custom_call_target="tpu_custom_call" | custom-call | flops 1073741824 | tf_op jit(solution)/shard_map/forward_away_near/pallas_call | solution.py:117
  21.8 0.2 collective-permute-start.5
  22.0 0.4 collective-permute-start.6
  22.4 3.6 %collective-permute-start.9 = (bf16[512,256]{1,0:T(8,128)(2,1)S(1)}, bf16[512,256]{1,0:T(8,128)(2,1)S(1)}, u32[]{:S(2)}, u32[]{:S(2)}) collective-permute-start(bf16[512,256]{1,0:T(8,128)(2,1)S(1)} %get-tuple-element.28.refs_5_), channel_id=1, source_target_pairs={{0,6},{1,7},{2,4},{3,5},{4,2},{5,3},{6,0},{7,1},{8,14},{9,15},{10,... | collective-permute-start | bytes 786440 | tf_op jit(solution)/shard_map/ppermute | solution.py:147
  26.0 0.0 collective-permute-start.8
  26.0 0.0 collective-permute-done.5.refs_4_
  26.0 0.0 collective-permute-done.6.refs_5_
  26.0 1.3 %forward_home_near.1 = (bf16[512,256]{1,0:T(8,128)(2,1)S(1)}, f32[512,256]{1,0:T(8,128)S(1)}) custom-call(bf16[4096,2048]{1,0:T(8,128)(2,1)S(1)} %load_tiles.1.adjacency_ref.refs_0_, bf16[512,256]{1,0:T(8,128)(2,1)S(1)} %copy-done, bf16[512,256]{1,0:T(8,128)(2,1)S(1)} %collective-permute-done.refs_1_.refs_2_, ...), custom_call_target="tpu_custom_call" | custom-call | flops 1073741824 | tf_op jit(solution)/shard_map/forward_home_near/pallas_call | solution.py:117
  27.3 0.8 collective-permute-start.7
  28.1 20.5 %collective-permute-done.8.r2_ref = bf16[512,256]{1,0:T(8,128)(2,1)S(1)} collective-permute-done((bf16[512,256]{1,0:T(8,128)(2,1)S(1)}, bf16[512,256]{1,0:T(8,128)(2,1)S(1)}, u32[]{:S(2)}, u32[]{:S(2)}) %collective-permute-start.8) | collective-permute-done | bytes 262176 | tf_op jit(solution)/shard_map/ppermute | solution.py:147
  48.6 0.0 collective-permute-done.9.r3_ref
  48.6 0.0 collective-permute-done.7.r1_ref
  48.6 1.1 %middle.1 = (bf16[512,256]{1,0:T(8,128)(2,1)}, bf16[512,256]{1,0:T(8,128)(2,1)S(1)}, f32[128,256]{1,0:T(8,128)S(1)}, f32[128,256]{1,0:T(8,128)S(1)}) custom-call(bf16[256,256]{1,0:T(8,128)(2,1)S(1)} %copy-done.2, bf16[512,256]{1,0:T(8,128)(2,1)S(1)} %copy-done.1, f32[512,256]{1,0:T(8,128)S(1)} %get-tuple-element.31.mine_ref, ...), custom_call_target="tpu_custom_call" | custom-call | tf_op jit(solution)/shard_map/middle/pallas_call | solution.py:117
  49.8 0.0 collective-permute-start.10
  49.8 0.0 collective-permute-start.15
  49.8 1.3 %collective-permute-done.15.other_ref = f32[128,256]{1,0:T(8,128)S(1)} collective-permute-done((f32[128,256]{1,0:T(8,128)S(1)}, f32[128,256]{1,0:T(8,128)S(1)}, u32[]{:S(2)}, u32[]{:S(2)}) %collective-permute-start.15) | collective-permute-done | bytes 131104 | tf_op jit(solution)/shard_map/ppermute | solution.py:147
  51.1 1.3 %collective-permute-start.16 = (f32[128,256]{1,0:T(8,128)S(1)}, f32[128,256]{1,0:T(8,128)S(1)}, u32[]{:S(2)}, u32[]{:S(2)}) collective-permute-start(f32[128,256]{1,0:T(8,128)S(1)} %weight_sum.5.mine_ref), channel_id=1, source_target_pairs={{0,8},{8,0},{16,24},{24,16},{1,9},{9,1},{17,25},{25,17},{2,10},{10... | collective-permute-start | bytes 393224 | tf_op jit(solution)/shard_map/ppermute | solution.py:147
  52.4 3.0 %collective-permute-start.13 = (bf16[512,256]{1,0:T(8,128)(2,1)S(1)}, bf16[512,256]{1,0:T(8,128)(2,1)S(1)}, u32[]{:S(2)}, u32[]{:S(2)}) collective-permute-start(bf16[512,256]{1,0:T(8,128)(2,1)S(1)} %get-tuple-element.35.refs_0_), channel_id=1, source_target_pairs={{0,4},{1,5},{2,6},{3,7},{4,0},{5,1},{6,2},{7,3},{8,12},{9,13},{10,... | collective-permute-start | bytes 786440 | tf_op jit(solution)/shard_map/ppermute | solution.py:147
  55.5 1.4 %collective-permute-start.14 = (bf16[512,256]{1,0:T(8,128)(2,1)S(1)}, bf16[512,256]{1,0:T(8,128)(2,1)S(1)}, u32[]{:S(2)}, u32[]{:S(2)}) collective-permute-start(bf16[512,256]{1,0:T(8,128)(2,1)S(1)} %get-tuple-element.35.refs_0_), channel_id=1, source_target_pairs={{0,6},{1,7},{2,4},{3,5},{4,2},{5,3},{6,0},{7,1},{8,14},{9,15},{10,... | collective-permute-start | bytes 786440 | tf_op jit(solution)/shard_map/ppermute | solution.py:147
  56.8 0.0 collective-permute-start.11
  56.8 2.3 %collective-permute-done.10.refs_1_ = bf16[512,256]{1,0:T(8,128)(2,1)S(1)} collective-permute-done((bf16[512,256]{1,0:T(8,128)(2,1)S(1)}, bf16[512,256]{1,0:T(8,128)(2,1)S(1)}, u32[]{:S(2)}, u32[]{:S(2)}) %collective-permute-start.10) | collective-permute-done | bytes 262176 | tf_op jit(solution)/shard_map/ppermute | solution.py:147
  59.1 0.0 collective-permute-start.12
  59.2 0.0 collective-permute-done.16.other_ref
  59.2 2.3 %collective-permute-start.17 = (f32[128,256]{1,0:T(8,128)S(1)}, f32[128,256]{1,0:T(8,128)S(1)}, u32[]{:S(2)}, u32[]{:S(2)}) collective-permute-start(f32[128,256]{1,0:T(8,128)S(1)} %weight_sum.6.mine_ref), channel_id=1, source_target_pairs={{0,16},{8,24},{16,0},{24,8},{1,17},{9,25},{17,1},{25,9},{2,18},{10... | collective-permute-start | bytes 393224 | tf_op jit(solution)/shard_map/ppermute | solution.py:147
  61.5 1.3 %backward_home.1.refs_2_.start_ref = f32[2048,256]{1,0:T(8,128)S(1)} custom-call(bf16[4096,2048]{1,0:T(8,128)(2,1)S(1)} %load_tiles.1.adjacency_ref.refs_0_, bf16[512,256]{1,0:T(8,128)(2,1)S(1)} %get-tuple-element.35.refs_0_, bf16[512,256]{1,0:T(8,128)(2,1)S(1)} %collective-permute-done.10.refs_1_), custom_call_target="tpu_custom_call" | custom-call | flops 1073741824 | tf_op jit(solution)/shard_map/backward_home/pallas_call | solution.py:117
  62.8 2.8 %collective-permute-done.17.other_ref = f32[128,256]{1,0:T(8,128)S(1)} collective-permute-done((f32[128,256]{1,0:T(8,128)S(1)}, f32[128,256]{1,0:T(8,128)S(1)}, u32[]{:S(2)}, u32[]{:S(2)}) %collective-permute-start.17) | collective-permute-done | bytes 131104 | tf_op jit(solution)/shard_map/ppermute | solution.py:147
  65.6 8.2 %collective-permute-done.13.refs_0_ = bf16[512,256]{1,0:T(8,128)(2,1)S(1)} collective-permute-done((bf16[512,256]{1,0:T(8,128)(2,1)S(1)}, bf16[512,256]{1,0:T(8,128)(2,1)S(1)}, u32[]{:S(2)}, u32[]{:S(2)}) %collective-permute-start.13) | collective-permute-done | bytes 262176 | tf_op jit(solution)/shard_map/ppermute | solution.py:147
  73.9 0.0 collective-permute-done.14.refs_1_
  73.9 0.0 collective-permute-start.18
  73.9 0.5 collective-permute-start.19
  74.4 5.4 %collective-permute-start.23 = (f32[128,256]{1,0:T(8,128)S(1)}, f32[128,256]{1,0:T(8,128)S(1)}, u32[]{:S(2)}, u32[]{:S(2)}) collective-permute-start(f32[128,256]{1,0:T(8,128)S(1)} %weight_sum.7.refs_3_.refs_0_), channel_id=1, source_target_pairs={{0,2},{1,3},{2,0},{3,1},{4,6},{5,7},{6,4},{7,5},{8,10},{9,11},{10,... | collective-permute-start | bytes 393224 | tf_op jit(solution)/shard_map/ppermute | solution.py:147
  79.8 0.0 collective-permute-done.11.refs_0_
  79.8 0.0 collective-permute-done.12.refs_1_
  79.8 2.4 %backward_most.1.start_ref.refs_1_ = f32[2048,256]{1,0:T(8,128)S(1)} custom-call(bf16[4096,2048]{1,0:T(8,128)(2,1)S(1)} %load_tiles.1.adjacency_ref.refs_0_, f32[2048,256]{1,0:T(8,128)S(1)} %backward_home.1.refs_2_.start_ref, bf16[512,256]{1,0:T(8,128)(2,1)S(1)} %collective-permute-done.11.refs_0_, bf16[512,256]{1,0:T(8,128)(2,1)S(1)} %collective-permute-done.12.refs_1_, ...), custom_call_target="tpu_custom_call" | custom-call | flops 2147483648 | tf_op jit(solution)/shard_map/backward_most/pallas_call | solution.py:117
  82.2 0.0 collective-permute-done.18.refs_0_.refs_2_
  82.2 0.0 collective-permute-done.19.refs_1_.refs_3_
  82.2 1.1 %backward_far_away.1 = (bf16[512,256]{1,0:T(8,128)(2,1)S(1)}, bf16[512,256]{1,0:T(8,128)(2,1)S(1)}, bf16[512,256]{1,0:T(8,128)(2,1)S(1)}) custom-call(bf16[4096,2048]{1,0:T(8,128)(2,1)S(1)} %load_tiles.1.adjacency_ref.refs_0_, f32[2048,256]{1,0:T(8,128)S(1)} %backward_most.1.start_ref.refs_1_, bf16[512,256]{1,0:T(8,128)(2,1)S(1)} %collective-permute-done.18.refs_0_.refs_2_, ...), custom_call_target="tpu_custom_call" | custom-call | flops 805306368 | tf_op jit(solution)/shard_map/backward_far_away/pallas_call | solution.py:117
  83.3 1.8 %collective-permute-start.20 = (bf16[512,256]{1,0:T(8,128)(2,1)S(1)}, bf16[512,256]{1,0:T(8,128)(2,1)S(1)}, u32[]{:S(2)}, u32[]{:S(2)}) collective-permute-start(bf16[512,256]{1,0:T(8,128)(2,1)S(1)} %get-tuple-element.40.refs_4_), channel_id=1, source_target_pairs={{0,24},{8,16},{16,8},{24,0},{1,25},{9,17},{17,9},{25,1},{2,26},{10... | collective-permute-start | bytes 786440 | tf_op jit(solution)/shard_map/ppermute | solution.py:147
  85.1 0.5 collective-permute-start.21
  85.6 0.5 backward_mine.1.refs_2_.mine_ref
  86.1 0.0 collective-permute-done.23.refs_1_
  86.2 0.7 collective-permute-start.24
  86.9 1.2 %collective-permute-start.22 = (bf16[512,256]{1,0:T(8,128)(2,1)S(1)}, bf16[512,256]{1,0:T(8,128)(2,1)S(1)}, u32[]{:S(2)}, u32[]{:S(2)}) collective-permute-start(bf16[512,256]{1,0:T(8,128)(2,1)S(1)} %get-tuple-element.42), channel_id=1, source_target_pairs={{0,8},{8,0},{16,24},{24,16},{1,9},{9,1},{17,25},{25,17},{2,10},{10... | collective-permute-start | bytes 786440 | tf_op jit(solution)/shard_map/ppermute | solution.py:147
  88.1 6.1 %collective-permute-done.24.other_ref = f32[128,256]{1,0:T(8,128)S(1)} collective-permute-done((f32[128,256]{1,0:T(8,128)S(1)}, f32[128,256]{1,0:T(8,128)S(1)}, u32[]{:S(2)}, u32[]{:S(2)}) %collective-permute-start.24) | collective-permute-done | bytes 131104 | tf_op jit(solution)/shard_map/ppermute | solution.py:147
  94.3 0.1 collective-permute-start.25
  94.3 0.0 collective-permute-done.20.q1_ref
  94.4 3.5 %collective-permute-done.21.q2_ref = bf16[512,256]{1,0:T(8,128)(2,1)S(1)} collective-permute-done((bf16[512,256]{1,0:T(8,128)(2,1)S(1)}, bf16[512,256]{1,0:T(8,128)(2,1)S(1)}, u32[]{:S(2)}, u32[]{:S(2)}) %collective-permute-start.21) | collective-permute-done | bytes 262176 | tf_op jit(solution)/shard_map/ppermute | solution.py:147
  97.8 0.9 finish.1
  (12 shorter events, 0.1 us)
Async XLA Ops:
  0.6 11.8 %collective-permute-start = (bf16[512,256]{1,0:T(8,128)(2,1)}, bf16[512,256]{1,0:T(8,128)(2,1)S(1)}, u32[]{:S(2)}, u32[]{:S(2)}) collective-permute-start(bf16[512,256]{1,0:T(8,128)(2,1)} %refs_0_.5), channel_id=1, source_target_pairs={{0,8},{8,0},{16,24},{24,16},{1,9},{9,1},{17,25},{25,17},{2,10},{10... | collective-permute-start | bytes 786440 | tf_op jit(solution)/shard_map/ppermute | solution.py:147
  3.6 13.6 %collective-permute-start.1 = (bf16[512,256]{1,0:T(8,128)(2,1)}, bf16[512,256]{1,0:T(8,128)(2,1)S(1)}, u32[]{:S(2)}, u32[]{:S(2)}) collective-permute-start(bf16[512,256]{1,0:T(8,128)(2,1)} %refs_0_.5), channel_id=1, source_target_pairs={{0,16},{8,24},{16,0},{24,8},{1,17},{9,25},{17,1},{25,9},{2,18},{10... | collective-permute-start | bytes 786440 | tf_op jit(solution)/shard_map/ppermute | solution.py:147
  5.2 12.1 %collective-permute-start.2 = (bf16[512,256]{1,0:T(8,128)(2,1)}, bf16[512,256]{1,0:T(8,128)(2,1)S(1)}, u32[]{:S(2)}, u32[]{:S(2)}) collective-permute-start(bf16[512,256]{1,0:T(8,128)(2,1)} %refs_0_.5), channel_id=1, source_target_pairs={{0,24},{8,16},{16,8},{24,0},{1,25},{9,17},{17,9},{25,1},{2,26},{10... | collective-permute-start | bytes 786440 | tf_op jit(solution)/shard_map/ppermute | solution.py:147
  5.8 11.4 %copy-start = (bf16[512,256]{1,0:T(8,128)(2,1)S(1)}, bf16[512,256]{1,0:T(8,128)(2,1)}, u32[]{:S(2)}) copy-start(bf16[512,256]{1,0:T(8,128)(2,1)} %refs_0_.5) | copy-start | bytes 786436
  18.5 1.8 %collective-permute-start.3 = (bf16[512,256]{1,0:T(8,128)(2,1)S(1)}, bf16[512,256]{1,0:T(8,128)(2,1)S(1)}, u32[]{:S(2)}, u32[]{:S(2)}) collective-permute-start(bf16[512,256]{1,0:T(8,128)(2,1)S(1)} %get-tuple-element.26), channel_id=1, source_target_pairs={{0,1},{1,0},{2,3},{3,2},{4,5},{5,4},{6,7},{7,6},{8,9},{9,8},{10,11... | collective-permute-start | bytes 786440 | tf_op jit(solution)/shard_map/ppermute | solution.py:147
  18.6 1.9 %collective-permute-start.4 = (bf16[512,256]{1,0:T(8,128)(2,1)S(1)}, bf16[512,256]{1,0:T(8,128)(2,1)S(1)}, u32[]{:S(2)}, u32[]{:S(2)}) collective-permute-start(bf16[512,256]{1,0:T(8,128)(2,1)S(1)} %get-tuple-element.27), channel_id=1, source_target_pairs={{0,1},{1,0},{2,3},{3,2},{4,5},{5,4},{6,7},{7,6},{8,9},{9,8},{10,11... | collective-permute-start | bytes 786440 | tf_op jit(solution)/shard_map/ppermute | solution.py:147
  20.6 28.1 %copy-start.1 = (bf16[512,256]{1,0:T(8,128)(2,1)S(1)}, bf16[512,256]{1,0:T(8,128)(2,1)}, u32[]{:S(2)}) copy-start(bf16[512,256]{1,0:T(8,128)(2,1)} %cotangent_ref.1) | copy-start | bytes 786436
  20.6 28.1 %copy-start.2 = (bf16[256,256]{1,0:T(8,128)(2,1)S(1)}, bf16[256,256]{1,0:T(8,128)(2,1)}, u32[]{:S(2)}) copy-start(bf16[256,256]{1,0:T(8,128)(2,1)} %weight_ref.1) | copy-start | bytes 393220
  21.8 4.2 %collective-permute-start.5 = (bf16[512,256]{1,0:T(8,128)(2,1)S(1)}, bf16[512,256]{1,0:T(8,128)(2,1)S(1)}, u32[]{:S(2)}, u32[]{:S(2)}) collective-permute-start(bf16[512,256]{1,0:T(8,128)(2,1)S(1)} %get-tuple-element.29), channel_id=1, source_target_pairs={{0,1},{1,0},{2,3},{3,2},{4,5},{5,4},{6,7},{7,6},{8,9},{9,8},{10,11... | collective-permute-start | bytes 786440 | tf_op jit(solution)/shard_map/ppermute | solution.py:147
  22.0 4.0 %collective-permute-start.6 = (bf16[512,256]{1,0:T(8,128)(2,1)S(1)}, bf16[512,256]{1,0:T(8,128)(2,1)S(1)}, u32[]{:S(2)}, u32[]{:S(2)}) collective-permute-start(bf16[512,256]{1,0:T(8,128)(2,1)S(1)} %get-tuple-element.30), channel_id=1, source_target_pairs={{0,1},{1,0},{2,3},{3,2},{4,5},{5,4},{6,7},{7,6},{8,9},{9,8},{10,11... | collective-permute-start | bytes 786440 | tf_op jit(solution)/shard_map/ppermute | solution.py:147
  22.4 26.2 %collective-permute-start.9 = (bf16[512,256]{1,0:T(8,128)(2,1)S(1)}, bf16[512,256]{1,0:T(8,128)(2,1)S(1)}, u32[]{:S(2)}, u32[]{:S(2)}) collective-permute-start(bf16[512,256]{1,0:T(8,128)(2,1)S(1)} %get-tuple-element.28.refs_5_), channel_id=1, source_target_pairs={{0,6},{1,7},{2,4},{3,5},{4,2},{5,3},{6,0},{7,1},{8,14},{9,15},{10,... | collective-permute-start | bytes 786440 | tf_op jit(solution)/shard_map/ppermute | solution.py:147
  26.0 22.6 %collective-permute-start.8 = (bf16[512,256]{1,0:T(8,128)(2,1)S(1)}, bf16[512,256]{1,0:T(8,128)(2,1)S(1)}, u32[]{:S(2)}, u32[]{:S(2)}) collective-permute-start(bf16[512,256]{1,0:T(8,128)(2,1)S(1)} %get-tuple-element.33), channel_id=1, source_target_pairs={{0,4},{1,5},{2,6},{3,7},{4,0},{5,1},{6,2},{7,3},{8,12},{9,13},{10,... | collective-permute-start | bytes 786440 | tf_op jit(solution)/shard_map/ppermute | solution.py:147
  27.3 21.3 %collective-permute-start.7 = (bf16[512,256]{1,0:T(8,128)(2,1)S(1)}, bf16[512,256]{1,0:T(8,128)(2,1)S(1)}, u32[]{:S(2)}, u32[]{:S(2)}) collective-permute-start(bf16[512,256]{1,0:T(8,128)(2,1)S(1)} %get-tuple-element.32), channel_id=1, source_target_pairs={{0,2},{1,3},{2,0},{3,1},{4,6},{5,7},{6,4},{7,5},{8,10},{9,11},{10,... | collective-permute-start | bytes 786440 | tf_op jit(solution)/shard_map/ppermute | solution.py:147
  49.8 9.4 %collective-permute-start.10 = (bf16[512,256]{1,0:T(8,128)(2,1)S(1)}, bf16[512,256]{1,0:T(8,128)(2,1)S(1)}, u32[]{:S(2)}, u32[]{:S(2)}) collective-permute-start(bf16[512,256]{1,0:T(8,128)(2,1)S(1)} %get-tuple-element.35.refs_0_), channel_id=1, source_target_pairs={{0,2},{1,3},{2,0},{3,1},{4,6},{5,7},{6,4},{7,5},{8,10},{9,11},{10,... | collective-permute-start | bytes 786440 | tf_op jit(solution)/shard_map/ppermute | solution.py:147
  49.8 1.3 %collective-permute-start.15 = (f32[128,256]{1,0:T(8,128)S(1)}, f32[128,256]{1,0:T(8,128)S(1)}, u32[]{:S(2)}, u32[]{:S(2)}) collective-permute-start(f32[128,256]{1,0:T(8,128)S(1)} %get-tuple-element.37), channel_id=1, source_target_pairs={{0,1},{1,0},{2,3},{3,2},{4,5},{5,4},{6,7},{7,6},{8,9},{9,8},{10,11... | collective-permute-start | bytes 393224 | tf_op jit(solution)/shard_map/ppermute | solution.py:147
  51.1 8.0 %collective-permute-start.16 = (f32[128,256]{1,0:T(8,128)S(1)}, f32[128,256]{1,0:T(8,128)S(1)}, u32[]{:S(2)}, u32[]{:S(2)}) collective-permute-start(f32[128,256]{1,0:T(8,128)S(1)} %weight_sum.5.mine_ref), channel_id=1, source_target_pairs={{0,8},{8,0},{16,24},{24,16},{1,9},{9,1},{17,25},{25,17},{2,10},{10... | collective-permute-start | bytes 393224 | tf_op jit(solution)/shard_map/ppermute | solution.py:147
  52.4 21.4 %collective-permute-start.13 = (bf16[512,256]{1,0:T(8,128)(2,1)S(1)}, bf16[512,256]{1,0:T(8,128)(2,1)S(1)}, u32[]{:S(2)}, u32[]{:S(2)}) collective-permute-start(bf16[512,256]{1,0:T(8,128)(2,1)S(1)} %get-tuple-element.35.refs_0_), channel_id=1, source_target_pairs={{0,4},{1,5},{2,6},{3,7},{4,0},{5,1},{6,2},{7,3},{8,12},{9,13},{10,... | collective-permute-start | bytes 786440 | tf_op jit(solution)/shard_map/ppermute | solution.py:147
  55.5 18.4 %collective-permute-start.14 = (bf16[512,256]{1,0:T(8,128)(2,1)S(1)}, bf16[512,256]{1,0:T(8,128)(2,1)S(1)}, u32[]{:S(2)}, u32[]{:S(2)}) collective-permute-start(bf16[512,256]{1,0:T(8,128)(2,1)S(1)} %get-tuple-element.35.refs_0_), channel_id=1, source_target_pairs={{0,6},{1,7},{2,4},{3,5},{4,2},{5,3},{6,0},{7,1},{8,14},{9,15},{10,... | collective-permute-start | bytes 786440 | tf_op jit(solution)/shard_map/ppermute | solution.py:147
  56.8 23.0 %collective-permute-start.11 = (bf16[512,256]{1,0:T(8,128)(2,1)S(1)}, bf16[512,256]{1,0:T(8,128)(2,1)S(1)}, u32[]{:S(2)}, u32[]{:S(2)}) collective-permute-start(bf16[512,256]{1,0:T(8,128)(2,1)S(1)} %get-tuple-element.35.refs_0_), channel_id=1, source_target_pairs={{0,1},{1,0},{2,3},{3,2},{4,5},{5,4},{6,7},{7,6},{8,9},{9,8},{10,11... | collective-permute-start | bytes 786440 | tf_op jit(solution)/shard_map/ppermute | solution.py:147
  59.1 20.6 %collective-permute-start.12 = (bf16[512,256]{1,0:T(8,128)(2,1)S(1)}, bf16[512,256]{1,0:T(8,128)(2,1)S(1)}, u32[]{:S(2)}, u32[]{:S(2)}) collective-permute-start(bf16[512,256]{1,0:T(8,128)(2,1)S(1)} %collective-permute-done.10.refs_1_), channel_id=1, source_target_pairs={{0,1},{1,0},{2,3},{3,2},{4,5},{5,4},{6,7},{7,6},{8,9},{9,8},{10,11... | collective-permute-start | bytes 786440 | tf_op jit(solution)/shard_map/ppermute | solution.py:147
  59.2 6.5 %collective-permute-start.17 = (f32[128,256]{1,0:T(8,128)S(1)}, f32[128,256]{1,0:T(8,128)S(1)}, u32[]{:S(2)}, u32[]{:S(2)}) collective-permute-start(f32[128,256]{1,0:T(8,128)S(1)} %weight_sum.6.mine_ref), channel_id=1, source_target_pairs={{0,16},{8,24},{16,0},{24,8},{1,17},{9,25},{17,1},{25,9},{2,18},{10... | collective-permute-start | bytes 393224 | tf_op jit(solution)/shard_map/ppermute | solution.py:147
  73.9 8.3 %collective-permute-start.18 = (bf16[512,256]{1,0:T(8,128)(2,1)S(1)}, bf16[512,256]{1,0:T(8,128)(2,1)S(1)}, u32[]{:S(2)}, u32[]{:S(2)}) collective-permute-start(bf16[512,256]{1,0:T(8,128)(2,1)S(1)} %get-tuple-element.38.refs_2_), channel_id=1, source_target_pairs={{0,1},{1,0},{2,3},{3,2},{4,5},{5,4},{6,7},{7,6},{8,9},{9,8},{10,11... | collective-permute-start | bytes 786440 | tf_op jit(solution)/shard_map/ppermute | solution.py:147
  73.9 8.3 %collective-permute-start.19 = (bf16[512,256]{1,0:T(8,128)(2,1)S(1)}, bf16[512,256]{1,0:T(8,128)(2,1)S(1)}, u32[]{:S(2)}, u32[]{:S(2)}) collective-permute-start(bf16[512,256]{1,0:T(8,128)(2,1)S(1)} %get-tuple-element.39.refs_3_), channel_id=1, source_target_pairs={{0,1},{1,0},{2,3},{3,2},{4,5},{5,4},{6,7},{7,6},{8,9},{9,8},{10,11... | collective-permute-start | bytes 786440 | tf_op jit(solution)/shard_map/ppermute | solution.py:147
  74.4 11.8 %collective-permute-start.23 = (f32[128,256]{1,0:T(8,128)S(1)}, f32[128,256]{1,0:T(8,128)S(1)}, u32[]{:S(2)}, u32[]{:S(2)}) collective-permute-start(f32[128,256]{1,0:T(8,128)S(1)} %weight_sum.7.refs_3_.refs_0_), channel_id=1, source_target_pairs={{0,2},{1,3},{2,0},{3,1},{4,6},{5,7},{6,4},{7,5},{8,10},{9,11},{10,... | collective-permute-start | bytes 393224 | tf_op jit(solution)/shard_map/ppermute | solution.py:147
  83.3 11.0 %collective-permute-start.20 = (bf16[512,256]{1,0:T(8,128)(2,1)S(1)}, bf16[512,256]{1,0:T(8,128)(2,1)S(1)}, u32[]{:S(2)}, u32[]{:S(2)}) collective-permute-start(bf16[512,256]{1,0:T(8,128)(2,1)S(1)} %get-tuple-element.40.refs_4_), channel_id=1, source_target_pairs={{0,24},{8,16},{16,8},{24,0},{1,25},{9,17},{17,9},{25,1},{2,26},{10... | collective-permute-start | bytes 786440 | tf_op jit(solution)/shard_map/ppermute | solution.py:147
  85.1 12.7 %collective-permute-start.21 = (bf16[512,256]{1,0:T(8,128)(2,1)S(1)}, bf16[512,256]{1,0:T(8,128)(2,1)S(1)}, u32[]{:S(2)}, u32[]{:S(2)}) collective-permute-start(bf16[512,256]{1,0:T(8,128)(2,1)S(1)} %get-tuple-element.41), channel_id=1, source_target_pairs={{0,16},{8,24},{16,0},{24,8},{1,17},{9,25},{17,1},{25,9},{2,18},{10... | collective-permute-start | bytes 786440 | tf_op jit(solution)/shard_map/ppermute | solution.py:147
  86.2 8.1 %collective-permute-start.24 = (f32[128,256]{1,0:T(8,128)S(1)}, f32[128,256]{1,0:T(8,128)S(1)}, u32[]{:S(2)}, u32[]{:S(2)}) collective-permute-start(f32[128,256]{1,0:T(8,128)S(1)} %weight_sum.8.mine_ref), channel_id=1, source_target_pairs={{0,4},{1,5},{2,6},{3,7},{4,0},{5,1},{6,2},{7,3},{8,12},{9,13},{10,... | collective-permute-start | bytes 393224 | tf_op jit(solution)/shard_map/ppermute | solution.py:147
  86.9 10.9 %collective-permute-start.22 = (bf16[512,256]{1,0:T(8,128)(2,1)S(1)}, bf16[512,256]{1,0:T(8,128)(2,1)S(1)}, u32[]{:S(2)}, u32[]{:S(2)}) collective-permute-start(bf16[512,256]{1,0:T(8,128)(2,1)S(1)} %get-tuple-element.42), channel_id=1, source_target_pairs={{0,8},{8,0},{16,24},{24,16},{1,9},{9,1},{17,25},{25,17},{2,10},{10... | collective-permute-start | bytes 786440 | tf_op jit(solution)/shard_map/ppermute | solution.py:147
  94.3 3.6 %collective-permute-start.25 = (f32[128,256]{1,0:T(8,128)S(1)}, f32[128,256]{1,0:T(8,128)S(1)}, u32[]{:S(2)}, u32[]{:S(2)}) collective-permute-start(f32[128,256]{1,0:T(8,128)S(1)} %weight_sum.9.half_ref), channel_id=1, source_target_pairs={{0,1},{1,0},{2,3},{3,2},{4,5},{5,4},{6,7},{7,6},{8,9},{9,8},{10,11... | collective-permute-start | bytes 393224 | tf_op jit(solution)/shard_map/ppermute | solution.py:147

commit v2 on v1

--- a/solution.py
+++ b/solution.py
@@ -107,6 +107,8 @@
     grad_weight = lax.psum(weight_term, ("row", "col"))
     return (activated, grad_features, grad_weight)
 
+COVER = 10**10
+
 
 def kernel_call(kernel, out_shape, arguments, name, flops=0, scratch=(), in_specs=None, after=()):
     count = len(arguments)
@@ -126,7 +128,7 @@
     )(*arguments, *after)
 
 
-def later(values, after):
+def later(values, after, flops=0):
     return pl.pallas_call(
         lambda *refs: None,
         out_shape=[jax.ShapeDtypeStruct(value.shape, value.dtype) for value in values],
@@ -134,6 +136,7 @@
         out_specs=[IN_PLACE] * len(values),
         input_output_aliases={i: i for i in range(len(values))},
         compiler_params=pltpu.CompilerParams(vmem_limit_bytes=VMEM_LIMIT),
+        cost_estimate=pl.CostEstimate(flops=flops, bytes_accessed=0, transcendentals=0),
         name="later",
     )(*values, *after)
 
@@ -179,14 +182,53 @@
 
 
 def forward_kernel(slots, adjacency_ref, *refs):
-    source = jnp.concatenate([ref[...] for ref in refs[:4]], axis=0)
+    source = jnp.concatenate([ref[...] for ref in refs[:3]], axis=0)
     others, out_refs = refs[4 : -len(slots)], refs[-len(slots) :]
     nodes = refs[0].shape[0]
     for i, slot in enumerate(slots):
-        total = jnp.dot(adjacency_ref[nodes * slot : nodes * (slot + 1), :], source, preferred_element_type=F32)
+        total = jnp.dot(adjacency_ref[nodes * slot : nodes * (slot + 1), nodes:], source, preferred_element_type=F32)
+        total = total + refs[3][nodes * slot : nodes * (slot + 1), :]
         if others:
             total = total + others[i][...].astype(F32)
         out_refs[i][...] = total.astype(out_refs[i].dtype)
+
+
+def forward_own_kernel(adjacency_ref, source_ref, out_ref):
+    nodes = source_ref.shape[0]
+    for top in range(0, out_ref.shape[0], nodes):
+        out_ref[top : top + nodes, :] = jnp.dot(
+            adjacency_ref[top : top + nodes, :nodes], source_ref[...], preferred_element_type=F32
+        )
+
+
+def forward_parts_kernel(slots, adjacency_ref, *refs):
+    *sources, own_ref = refs[:4]
+    source = jnp.concatenate([ref[...] for ref in sources], axis=0)
+    nodes = sources[0].shape[0]
+    out_refs = refs[4:]
+    size = out_refs[0].shape[0]
+    for i, out_ref in enumerate(out_refs):
+        top = nodes * slots[i * size // nodes] + i * size % nodes
+        total = jnp.dot(adjacency_ref[top : top + size, nodes:], source, preferred_element_type=F32)
+        out_ref[...] = (total + own_ref[top : top + size, :]).astype(out_ref.dtype)
+
+
+def forward_home_kernel(adjacency_ref, *refs):
+    *sources, own_ref = refs[:4]
+    others, near_refs, mine_ref = refs[4:-3], refs[-3:-1], refs[-1]
+    source = jnp.concatenate([ref[...] for ref in sources], axis=0)
+    nodes = sources[0].shape[0]
+
+    def total(slot, others):
+        here = slice(nodes * slot, nodes * (slot + 1))
+        value = jnp.dot(adjacency_ref[here, nodes:], source, preferred_element_type=F32) + own_ref[here, :]
+        return value + jnp.concatenate([ref[...] for ref in others], axis=0).astype(F32)
+
+    near = total(2, others[: len(others) // 2]).astype(BF16)
+    size = near_refs[0].shape[0]
+    for i, near_ref in enumerate(near_refs):
+        near_ref[...] = near[size * i : size * (i + 1), :]
+    mine_ref[...] = total(0, others[len(others) // 2 :])
 
 
 def add_kernel(*refs):
@@ -195,9 +237,14 @@
         out[...] = (mine[...] + other[...].astype(F32)).astype(out.dtype)
 
 
-def middle_kernel(weight_ref, cotangent_ref, mine_ref, r1_ref, r2_ref, r3_ref,
-                  activated_ref, sent_ref, keep_ref, send_ref, term_ref):
-    mixed = mine_ref[...] + r1_ref[...].astype(F32) + r2_ref[...].astype(F32) + r3_ref[...].astype(F32)
+def join_kernel(a_ref, b_ref, out_ref):
+    out_ref[...] = a_ref[...].astype(F32) + b_ref[...].astype(F32)
+
+
+def middle_kernel(weight_ref, cotangent_ref, mine_ref, far_ref, *refs):
+    *near_refs, activated_ref, sent_ref, mixed_ref, slope_ref = refs
+    near = jnp.concatenate([ref[...] for ref in near_refs], axis=0)
+    mixed = mine_ref[...] + near.astype(F32) + far_ref[...]
     mixed = mixed.astype(BF16)
     weight = weight_ref[...]
     summed = jnp.dot(mixed, weight, preferred_element_type=F32)
@@ -208,11 +255,18 @@
     sent_ref[...] = lax.dot_general(
         slope, weight, (((1,), (1,)), ((), ())), preferred_element_type=F32
     ).astype(BF16)
-    term_ref[...] = lax.dot_general(mixed, slope, (((0,), (0,)), ((), ())), preferred_element_type=F32)
+    mixed_ref[...] = mixed
+    slope_ref[...] = slope
+
+
+def term_kernel(mixed_ref, slope_ref, keep_ref, send_ref, term_ref):
+    term_ref[...] = lax.dot_general(
+        mixed_ref[...], slope_ref[...], (((0,), (0,)), ((), ())), preferred_element_type=F32
+    )
     half = keep_ref.shape[0]
     core = lax.axis_index("col") % 2
     keep_ref[...] = term_ref[pl.ds(pl.multiple_of(core * half, half), half), :]
-    send_ref[...] = term_ref[pl.ds(pl.multiple_of((1 - core) * half, half), half), :]
+    send_ref[...] = term_ref[pl.ds(pl.multiple_of((1 - core) * half, half), half), :].astype(send_ref.dtype)
 
 
 def backward_block(slots, chunk, nodes, adjacency_ref, source):
@@ -259,7 +313,7 @@
 
 
 def sum_kernel(mine_ref, other_ref, out_ref):
-    out_ref[...] = mine_ref[...] + other_ref[...]
+    out_ref[...] = (mine_ref[...].astype(F32) + other_ref[...].astype(F32)).astype(out_ref.dtype)
 
 
 def dense_body(features, weight, tile_values, tile_row, tile_col, tile_count, cotangent):
@@ -268,9 +322,12 @@
     rows, cols = nodes * lax.axis_size("col"), nodes * lax.axis_size("row")
     block = jax.ShapeDtypeStruct((nodes, hidden), BF16)
     exact = pltpu.VMEM((nodes, hidden), F32)
+
+    def part_of(count):
+        return jax.ShapeDtypeStruct((nodes // count, hidden), BF16)
+
     running = pltpu.VMEM((cols, hidden), F32)
     whole, half = (jax.ShapeDtypeStruct((hidden // n, hidden), F32) for n in (1, 2))
-    slot_flops = 2 * nodes * cols * hidden
 
     def in_hbm(value):
         return pltpu.with_memory_space_constraint(value, pltpu.HBM)
@@ -290,57 +347,73 @@
         in_specs=[IN_SMEM, IN_PLACE, IN_PLACE, IN_PLACE],
     )
     adjacency = held(adjacency)
-    source = [features] + [swap(features, "row", d) for d in (1, 2, 3)]
+    source = [swap(features, "row", d) for d in (1, 2, 3)]
+    own = kernel_call(
+        forward_own_kernel, pltpu.VMEM((rows, hidden), F32), (adjacency, features), "forward_own"
+    )
+    source.append(held(own))
 
     def forward(slot_ids, kind, name, others=(), after=()):
         return kernel_call(
             functools.partial(forward_kernel, slot_ids), [kind] * len(slot_ids) if not isinstance(kind, list) else kind,
-            (adjacency, *source, *others), name, flops=slot_flops * len(slot_ids), after=after,
+            (adjacency, *source, *others), name, after=after,
         )
 
     away_far = [swap(value, "col", 1) for value in forward((7, 5), block, "forward_away_far")]
     home_far = [held(value) for value in forward((6, 4), exact, "forward_home_far")]
     far = kernel_call(add_kernel, [block] * 2, (*home_far, *away_far), "add_far")
-    away_near = forward((3, 1), block, "forward_away_near", after=(far[0],))
+    away_near = kernel_call(
+        functools.partial(forward_parts_kernel, (3, 1)), [part_of(4)] * (2 * 4), (adjacency, *source), "forward_away_near",
+        after=(far[0],),
+    )
     away_near = [swap(value, "col", 1) for value in away_near]
     r3, r2 = swap(far[0], "col", 6), swap(far[1], "col", 4)
-    near, mine = forward((2, 0), [block, exact], "forward_home_near", others=away_near)
-    r1 = swap(near, "col", 2)
-    activated, sent, keep, send = kernel_call(
-        middle_kernel, [block, block, half, half], (weight, cotangent, held(mine), r1, r2, r3), "middle",
-        scratch=(pltpu.VMEM(whole.shape, F32),),
-    )
-
+    *near, mine = kernel_call(
+        forward_home_kernel, [part_of(2)] * 2 + [exact], (adjacency, *source, *away_near), "forward_home_near"
+    )
+    near = [swap(value, "col", 2) for value in near]
+    joined = kernel_call(join_kernel, exact, (r2, r3), "join_far", flops=COVER)
+    activated, sent, mixed, slope = kernel_call(
+        middle_kernel, [block] * 4, (weight, cotangent, held(mine), held(joined), *near), "middle"
+    )
     s3, s2, s1 = (swap(sent, "col", 2 * d) for d in (3, 2, 1))
     o0, o1 = swap(sent, "col", 1), swap(s1, "col", 1)
 
-    def add(value, axis, distance, after=()):
-        return kernel_call(sum_kernel, half, (value, swap(value, axis, distance)), "weight_sum", after=after)
-
-    term = kernel_call(sum_kernel, half, (keep, swap(send, "col", 1)), "weight_sum")
-    term = add(term, "row", 1)
-    term = add(term, "row", 2)
+    def add(value, axis, distance, dtype, after=()):
+        out_shape = jax.ShapeDtypeStruct(value.shape, dtype)
+        return kernel_call(sum_kernel, out_shape, (value, swap(value, axis, distance)), "weight_sum", after=after)
+
+    short = jax.ShapeDtypeStruct(half.shape, BF16)
+    keep, send = kernel_call(
+        term_kernel, [half, short], (mixed, slope), "weight_term", scratch=(pltpu.VMEM(whole.shape, F32),)
+    )
+    term = kernel_call(sum_kernel, short, (keep, swap(send, "col", 1)), "weight_sum")
+    term = add(term, "row", 1, BF16)
+    term = add(term, "row", 2, BF16)
+    term = add(term, "col", 2, BF16)
     start = kernel_call(
-        functools.partial(backward_near_kernel, (0, 2)), running, (adjacency, sent, s1),
-        "backward_home", flops=2 * slot_flops,
-    )
-    s2, s3 = later((s2, s3), (start, term))
+        functools.partial(backward_near_kernel, (0, 1, 2)), running, (adjacency, sent, o0, s1),
+        "backward_home",
+    )
+    s3, s2 = later((s3, s2), (start,), COVER)
+    s3, s2 = later((s3, s2), (term,))
     o2, o3 = swap(s2, "col", 1), swap(s3, "col", 1)
     start = kernel_call(
-        functools.partial(backward_home_kernel, (1, 3, 4, 6)), running, (adjacency, held(start), o0, o1, s2, s3),
-        "backward_most", flops=4 * slot_flops,
-    )
-    shares = kernel_call(
-        functools.partial(backward_away_kernel, (5, 7), (3, 2, 1)), [block] * 3,
-        (adjacency, held(start), o2, o3), "backward_far_away", flops=3 * slot_flops // 2,
-    )
+        functools.partial(backward_home_kernel, (3, 4, 6)), running, (adjacency, held(start), o1, s2, s3),
+        "backward_most",
+    )
+    shares = []
+    for chunks in ((3,), (2, 1)):
+        shares += kernel_call(
+            functools.partial(backward_away_kernel, (5, 7), chunks), [block] * len(chunks),
+            (adjacency, held(start), o2, o3), "backward_far_away", after=tuple(shares),
+        )
     returned = [swap(share, "row", d) for share, d in zip(shares, (3, 2, 1))]
     mine = kernel_call(
         functools.partial(backward_away_kernel, (5, 7), (0,)), [exact],
-        (adjacency, held(start), o2, o3), "backward_mine", flops=slot_flops // 2, after=(shares[0],),
+        (adjacency, held(start), o2, o3), "backward_mine", after=(shares[0],),
     )[0]
-    term = add(term, "col", 2, after=(mine,))
-    term = add(term, "col", 4)
+    term = add(later((term,), (mine,))[0], "col", 4, F32)
     grad_features, grad_weight = kernel_call(
         finish_kernel, [block, whole], (held(mine), *returned, term, swap(term, "col", 1)), "finish"
     )

time: 98.9 us -> 92.5 us (0.935)
  the two profiles are of different devices: /device:TPU:0 before, /device:TPU:21 now
where the time goes in v2:
time: 92.5 us; the launch traced here: 92.3 us
  waiting for transfers between devices  43.5 us (47%)
  starting transfers between devices  27.6 us (30%)
  Pallas kernels  19.6 us (21%)
  between operations  1.52 us (2%)
    ppermute x33, waiting for transfers between devices, swap(): return lax.ppermute(value, axis, [(i, i ^ distance) for i in range(count)])  43.5 us
    ppermute x33, starting transfers between devices, swap(): return lax.ppermute(value, axis, [(i, i ^ distance) for i in range(count)])  27.6 us
    pallas_call x21, Pallas kernels, kernel_call(): pl.pallas_call(ordered if after else kernel, out_shape=out_shape, in_spec...  19.6 us
  transfers between devices with their start and end apart: 33, of which 16 were waited for; matrix products, arithmetic and copies ran while one was open for 0% of the time, Pallas kernels for 17%

profile of v2, /device:TPU:21, one launch (start us, length us, event | category | flops | bytes accessed | tf_op | source)
XLA Modules:
  0.0 92.3 jit_solution(13373486128369068674)
XLA Ops:
  0.6 0.3 collective-permute-start.1
  0.9 1.2 %collective-permute-start = (bf16[512,256]{1,0:T(8,128)(2,1)}, bf16[512,256]{1,0:T(8,128)(2,1)S(1)}, u32[]{:S(2)}, u32[]{:S(2)}) collective-permute-start(bf16[512,256]{1,0:T(8,128)(2,1)} %source_ref.1), channel_id=1, source_target_pairs={{0,8},{8,0},{16,24},{24,16},{1,9},{9,1},{17,25},{25,17},{2,10},{10... | collective-permute-start | bytes 786440 | tf_op jit(solution)/shard_map/ppermute | solution.py:150
  2.1 1.2 %collective-permute-start.2 = (bf16[512,256]{1,0:T(8,128)(2,1)}, bf16[512,256]{1,0:T(8,128)(2,1)S(1)}, u32[]{:S(2)}, u32[]{:S(2)}) collective-permute-start(bf16[512,256]{1,0:T(8,128)(2,1)} %source_ref.1), channel_id=1, source_target_pairs={{0,24},{8,16},{16,8},{24,0},{1,25},{9,17},{17,9},{25,1},{2,26},{10... | collective-permute-start | bytes 786440 | tf_op jit(solution)/shard_map/ppermute | solution.py:150
  4.0 6.4 %load_tiles.1.adjacency_ref.refs_0_ = bf16[4096,2048]{1,0:T(8,128)(2,1)S(1)} custom-call(s32[1,1]{1,0:T(1,128)S(6)} %copy.20.count_ref, s32[512]{0:T(512)} %row_ref.1, s32[512]{0:T(512)} %col_ref.1, bf16[512,128,128]{2,1,0:T(8,128)(2,1)} %tiles_ref.1), custom_call_target="tpu_custom_call" | custom-call | tf_op jit(solution)/shard_map/load_tiles/pallas_call | solution.py:119
  10.4 1.3 %forward_own.1.refs_3_.refs_4_ = f32[4096,256]{1,0:T(8,128)S(1)} custom-call(bf16[4096,2048]{1,0:T(8,128)(2,1)S(1)} %load_tiles.1.adjacency_ref.refs_0_, bf16[512,256]{1,0:T(8,128)(2,1)S(1)} %copy-done.1), custom_call_target="tpu_custom_call" | custom-call | tf_op jit(solution)/shard_map/forward_own/pallas_call | solution.py:119
  11.7 2.9 %collective-permute-done.2.refs_2_.refs_3_ = bf16[512,256]{1,0:T(8,128)(2,1)S(1)} collective-permute-done((bf16[512,256]{1,0:T(8,128)(2,1)}, bf16[512,256]{1,0:T(8,128)(2,1)S(1)}, u32[]{:S(2)}, u32[]{:S(2)}) %collective-permute-start.2) | collective-permute-done | bytes 262176 | tf_op jit(solution)/shard_map/ppermute | solution.py:150
  14.6 1.0 %forward_away_far.1 = (bf16[512,256]{1,0:T(8,128)(2,1)S(1)}, bf16[512,256]{1,0:T(8,128)(2,1)S(1)}) custom-call(bf16[4096,2048]{1,0:T(8,128)(2,1)S(1)} %load_tiles.1.adjacency_ref.refs_0_, bf16[512,256]{1,0:T(8,128)(2,1)S(1)} %collective-permute-done.refs_0_.refs_1_, bf16[512,256]{1,0:T(8,128)(2,1)S(1)} %collective-permute-done.1.refs_1_.refs_2_, ...), custom_call_target="tpu_custom_call" | custom-call | tf_op jit(solution)/shard_map/forward_away_far/pallas_call | solution.py:119
  15.6 1.9 %collective-permute-start.3 = (bf16[512,256]{1,0:T(8,128)(2,1)S(1)}, bf16[512,256]{1,0:T(8,128)(2,1)S(1)}, u32[]{:S(2)}, u32[]{:S(2)}) collective-permute-start(bf16[512,256]{1,0:T(8,128)(2,1)S(1)} %get-tuple-element.36), channel_id=1, source_target_pairs={{0,1},{1,0},{2,3},{3,2},{4,5},{5,4},{6,7},{7,6},{8,9},{9,8},{10,11... | collective-permute-start | bytes 786440 | tf_op jit(solution)/shard_map/ppermute | solution.py:150
  17.5 0.1 collective-permute-start.4
  17.6 1.0 %forward_home_far.1 = (f32[512,256]{1,0:T(8,128)S(1)}, f32[512,256]{1,0:T(8,128)S(1)}) custom-call(bf16[4096,2048]{1,0:T(8,128)(2,1)S(1)} %load_tiles.1.adjacency_ref.refs_0_, bf16[512,256]{1,0:T(8,128)(2,1)S(1)} %collective-permute-done.refs_0_.refs_1_, bf16[512,256]{1,0:T(8,128)(2,1)S(1)} %collective-permute-done.1.refs_1_.refs_2_, ...), custom_call_target="tpu_custom_call" | custom-call | tf_op jit(solution)/shard_map/forward_home_far/pallas_call | solution.py:119
  18.5 0.1 collective-permute-done.3.refs_2_
  18.6 0.4 collective-permute-done.4.refs_3_
  19.0 0.1 add_far.1
  19.1 0.1 collective-permute-start.13
  19.2 2.4 %collective-permute-start.14 = (bf16[512,256]{1,0:T(8,128)(2,1)S(1)}, bf16[512,256]{1,0:T(8,128)(2,1)S(1)}, u32[]{:S(2)}, u32[]{:S(2)}) collective-permute-start(bf16[512,256]{1,0:T(8,128)(2,1)S(1)} %get-tuple-element.38.refs_5_), channel_id=1, source_target_pairs={{0,6},{1,7},{2,4},{3,5},{4,2},{5,3},{6,0},{7,1},{8,14},{9,15},{10,... | collective-permute-start | bytes 786440 | tf_op jit(solution)/shard_map/ppermute | solution.py:150
  21.7 1.0 %forward_away_near.1 = (bf16[128,256]{1,0:T(8,128)(2,1)S(1)}, bf16[128,256]{1,0:T(8,128)(2,1)S(1)}, bf16[128,256]{1,0:T(8,128)(2,1)S(1)}, bf16[128,256]{1,0:T(8,...) custom-call(bf16[4096,2048]{1,0:T(8,128)(2,1)S(1)} %load_tiles.1.adj, ...), custom_call_target="tpu_custom_call" | custom-call | tf_op jit(solution)/shard_map/forward_away_near/pallas_call | solution.py:119
  22.7 1.0 %collective-permute-start.5 = (bf16[128,256]{1,0:T(8,128)(2,1)S(1)}, bf16[128,256]{1,0:T(8,128)(2,1)S(1)}, u32[]{:S(2)}, u32[]{:S(2)}) collective-permute-start(bf16[128,256]{1,0:T(8,128)(2,1)S(1)} %get-tuple-element.39), channel_id=1, source_target_pairs={{0,1},{1,0},{2,3},{3,2},{4,5},{5,4},{6,7},{7,6},{8,9},{9,8},{10,11... | collective-permute-start | bytes 196616 | tf_op jit(solution)/shard_map/ppermute | solution.py:150
  23.7 0.1 collective-permute-start.6
  23.7 0.4 collective-permute-start.7
  24.2 0.4 collective-permute-done.5.refs_4_
  24.6 0.4 collective-permute-start.8
  24.9 0.2 collective-permute-start.9
  25.1 0.4 collective-permute-start.10
  25.4 0.4 collective-permute-done.8.refs_7_
  25.8 0.4 collective-permute-start.11
  26.2 0.2 collective-permute-start.12
  26.3 0.7 collective-permute-done.11.refs_10_
  27.1 0.4 collective-permute-done.12.refs_11_
  27.4 1.0 %forward_home_near.1 = (bf16[256,256]{1,0:T(8,128)(2,1)S(1)}, bf16[256,256]{1,0:T(8,128)(2,1)S(1)}, f32[512,256]{1,0:T(8,128)S(1)}) custom-call(bf16[4096,2048]{1,0:T(8,128)(2,1)S(1)} %load_tiles.1.adjacency_ref.refs_0_, bf16[512,256]{1,0:T(8,128)(2,1)S(1)} %collective-permute-done.refs_0_.refs_1_, ...), custom_call_target="tpu_custom_call" | custom-call | tf_op jit(solution)/shard_map/forward_home_near/pallas_call | solution.py:119
  28.4 1.1 %collective-permute-start.15 = (bf16[256,256]{1,0:T(8,128)(2,1)S(1)}, bf16[256,256]{1,0:T(8,128)(2,1)S(1)}, u32[]{:S(2)}, u32[]{:S(2)}) collective-permute-start(bf16[256,256]{1,0:T(8,128)(2,1)S(1)} %get-tuple-element.49), channel_id=1, source_target_pairs={{0,2},{1,3},{2,0},{3,1},{4,6},{5,7},{6,4},{7,5},{8,10},{9,11},{10,... | collective-permute-start | bytes 393224 | tf_op jit(solution)/shard_map/ppermute | solution.py:150
  29.5 0.4 collective-permute-start.16
  30.0 5.9 %collective-permute-done.13.a_ref = bf16[512,256]{1,0:T(8,128)(2,1)S(1)} collective-permute-done((bf16[512,256]{1,0:T(8,128)(2,1)S(1)}, bf16[512,256]{1,0:T(8,128)(2,1)S(1)}, u32[]{:S(2)}, u32[]{:S(2)}) %collective-permute-start.13) | collective-permute-done | bytes 262176 | tf_op jit(solution)/shard_map/ppermute | solution.py:150
  35.8 9.4 %collective-permute-done.14.b_ref = bf16[512,256]{1,0:T(8,128)(2,1)S(1)} collective-permute-done((bf16[512,256]{1,0:T(8,128)(2,1)S(1)}, bf16[512,256]{1,0:T(8,128)(2,1)S(1)}, u32[]{:S(2)}, u32[]{:S(2)}) %collective-permute-start.14) | collective-permute-done | bytes 262176 | tf_op jit(solution)/shard_map/ppermute | solution.py:150
  45.2 0.1 join_far.1.far_ref
  45.3 1.1 %middle.1 = (bf16[512,256]{1,0:T(8,128)(2,1)}, bf16[512,256]{1,0:T(8,128)(2,1)S(1)}, bf16[512,256]{1,0:T(8,128)(2,1)S(1)}, bf16[512,256]{1,0:T(8,128)(2,1)S(1)}) custom-call(bf16[256,256]{1,0:T(8,128)(2,1)S(1)} %copy-done.2, bf16[512,256]{1,0:T(8,128)(2,1)S(1)} %copy-done, f32[512,256]{1,0:T(8,128)S(1)} %get-tuple-element.47.mine_ref, ...), custom_call_target="tpu_custom_call" | custom-call | tf_op jit(solution)/shard_map/middle/pallas_call | solution.py:119
  46.4 1.1 %collective-permute-start.18 = (bf16[512,256]{1,0:T(8,128)(2,1)S(1)}, bf16[512,256]{1,0:T(8,128)(2,1)S(1)}, u32[]{:S(2)}, u32[]{:S(2)}) collective-permute-start(bf16[512,256]{1,0:T(8,128)(2,1)S(1)} %get-tuple-element.52.refs_0_), channel_id=1, source_target_pairs={{0,2},{1,3},{2,0},{3,1},{4,6},{5,7},{6,4},{7,5},{8,10},{9,11},{10,... | collective-permute-start | bytes 786440 | tf_op jit(solution)/shard_map/ppermute | solution.py:150
  47.5 0.7 collective-permute-start.17
  48.2 1.6 %collective-permute-start.20 = (bf16[512,256]{1,0:T(8,128)(2,1)S(1)}, bf16[512,256]{1,0:T(8,128)(2,1)S(1)}, u32[]{:S(2)}, u32[]{:S(2)}) collective-permute-start(bf16[512,256]{1,0:T(8,128)(2,1)S(1)} %get-tuple-element.52.refs_0_), channel_id=1, source_target_pairs={{0,6},{1,7},{2,4},{3,5},{4,2},{5,3},{6,0},{7,1},{8,14},{9,15},{10,... | collective-permute-start | bytes 786440 | tf_op jit(solution)/shard_map/ppermute | solution.py:150
  49.8 0.3 weight_term.1
  50.1 0.6 collective-permute-start.22
  50.8 0.9 collective-permute-done.22.other_ref
  51.7 1.3 %collective-permute-start.23 = (bf16[128,256]{1,0:T(8,128)(2,1)S(1)}, bf16[128,256]{1,0:T(8,128)(2,1)S(1)}, u32[]{:S(2)}, u32[]{:S(2)}) collective-permute-start(bf16[128,256]{1,0:T(8,128)(2,1)S(1)} %weight_sum.5.mine_ref), channel_id=1, source_target_pairs={{0,8},{8,0},{16,24},{24,16},{1,9},{9,1},{17,25},{25,17},{2,10},{10... | collective-permute-start | bytes 196616 | tf_op jit(solution)/shard_map/ppermute | solution.py:150
  53.0 2.2 %collective-permute-done.23.other_ref = bf16[128,256]{1,0:T(8,128)(2,1)S(1)} collective-permute-done((bf16[128,256]{1,0:T(8,128)(2,1)S(1)}, bf16[128,256]{1,0:T(8,128)(2,1)S(1)}, u32[]{:S(2)}, u32[]{:S(2)}) %collective-permute-start.23) | collective-permute-done | bytes 65568 | tf_op jit(solution)/shard_map/ppermute | solution.py:150
  55.2 0.3 collective-permute-start.24
  55.5 3.2 %collective-permute-done.24.other_ref = bf16[128,256]{1,0:T(8,128)(2,1)S(1)} collective-permute-done((bf16[128,256]{1,0:T(8,128)(2,1)S(1)}, bf16[128,256]{1,0:T(8,128)(2,1)S(1)}, u32[]{:S(2)}, u32[]{:S(2)}) %collective-permute-start.24) | collective-permute-done | bytes 65568 | tf_op jit(solution)/shard_map/ppermute | solution.py:150
  58.7 2.0 %collective-permute-start.25 = (bf16[128,256]{1,0:T(8,128)(2,1)S(1)}, bf16[128,256]{1,0:T(8,128)(2,1)S(1)}, u32[]{:S(2)}, u32[]{:S(2)}) collective-permute-start(bf16[128,256]{1,0:T(8,128)(2,1)S(1)} %weight_sum.7.mine_ref), channel_id=1, source_target_pairs={{0,2},{1,3},{2,0},{3,1},{4,6},{5,7},{6,4},{7,5},{8,10},{9,11},{10,... | collective-permute-start | bytes 196616 | tf_op jit(solution)/shard_map/ppermute | solution.py:150
  60.7 2.3 %collective-permute-start.19 = (bf16[512,256]{1,0:T(8,128)(2,1)S(1)}, bf16[512,256]{1,0:T(8,128)(2,1)S(1)}, u32[]{:S(2)}, u32[]{:S(2)}) collective-permute-start(bf16[512,256]{1,0:T(8,128)(2,1)S(1)} %collective-permute-done.18.refs_2_), channel_id=1, source_target_pairs={{0,1},{1,0},{2,3},{3,2},{4,5},{5,4},{6,7},{7,6},{8,9},{9,8},{10,11... | collective-permute-start | bytes 786440 | tf_op jit(solution)/shard_map/ppermute | solution.py:150
  63.0 1.9 %backward_home.1.refs_2_.start_ref = f32[2048,256]{1,0:T(8,128)S(1)} custom-call(bf16[4096,2048]{1,0:T(8,128)(2,1)S(1)} %load_tiles.1.adjacency_ref.refs_0_, bf16[512,256]{1,0:T(8,128)(2,1)S(1)} %get-tuple-element.52.refs_0_, bf16[512,256]{1,0:T(8,128)(2,1)S(1)} %collective-permute-done.17.refs_1_, bf16[512,256]{1,0:T(8,128)(2,1)S(1)} %collective-permute-done.18.refs_2_), custom_call_target="tpu_custom_call" | custom-call | tf_op jit(solution)/shard_map/backward_home/pallas_call | solution.py:119
  64.9 8.3 %collective-permute-done.20.refs_0_ = bf16[512,256]{1,0:T(8,128)(2,1)S(1)} collective-permute-done((bf16[512,256]{1,0:T(8,128)(2,1)S(1)}, bf16[512,256]{1,0:T(8,128)(2,1)S(1)}, u32[]{:S(2)}, u32[]{:S(2)}) %collective-permute-start.20) | collective-permute-done | bytes 262176 | tf_op jit(solution)/shard_map/ppermute | solution.py:150
  73.3 0.8 collective-permute-start.26
  74.1 0.1 collective-permute-start.27
  74.2 1.9 %backward_most.1.start_ref.refs_1_ = f32[2048,256]{1,0:T(8,128)S(1)} custom-call(bf16[4096,2048]{1,0:T(8,128)(2,1)S(1)} %load_tiles.1.adjacency_ref.refs_0_, f32[2048,256]{1,0:T(8,128)S(1)} %backward_home.1.refs_2_.start_ref, bf16[512,256]{1,0:T(8,128)(2,1)S(1)} %collective-permute-done.19.refs_0_, bf16[512,256]{1,0:T(8,128)(2,1)S(1)} %get-tuple-element.59.refs_1_, ...), custom_call_target="tpu_custom_call" | custom-call | tf_op jit(solution)/shard_map/backward_most/pallas_call | solution.py:119
  76.1 0.5 backward_far_away.2.refs_4_
  76.6 1.2 %collective-permute-start.28 = (bf16[512,256]{1,0:T(8,128)(2,1)S(1)}, bf16[512,256]{1,0:T(8,128)(2,1)S(1)}, u32[]{:S(2)}, u32[]{:S(2)}) collective-permute-start(bf16[512,256]{1,0:T(8,128)(2,1)S(1)} %backward_far_away.2.refs_4_), channel_id=1, source_target_pairs={{0,24},{8,16},{16,8},{24,0},{1,25},{9,17},{17,9},{25,1},{2,26},{10... | collective-permute-start | bytes 786440 | tf_op jit(solution)/shard_map/ppermute | solution.py:150
  77.8 0.8 backward_far_away.3
  78.6 1.3 %collective-permute-start.29 = (bf16[512,256]{1,0:T(8,128)(2,1)S(1)}, bf16[512,256]{1,0:T(8,128)(2,1)S(1)}, u32[]{:S(2)}, u32[]{:S(2)}) collective-permute-start(bf16[512,256]{1,0:T(8,128)(2,1)S(1)} %get-tuple-element.61), channel_id=1, source_target_pairs={{0,16},{8,24},{16,0},{24,8},{1,17},{9,25},{17,1},{25,9},{2,18},{10... | collective-permute-start | bytes 786440 | tf_op jit(solution)/shard_map/ppermute | solution.py:150
  79.9 0.3 collective-permute-start.30
  80.2 0.5 backward_mine.1.refs_1_.mine_ref
  80.7 0.1 collective-permute-start.31
  80.8 4.3 %collective-permute-done.31.other_ref = bf16[128,256]{1,0:T(8,128)(2,1)S(1)} collective-permute-done((bf16[128,256]{1,0:T(8,128)(2,1)S(1)}, bf16[128,256]{1,0:T(8,128)(2,1)S(1)}, u32[]{:S(2)}, u32[]{:S(2)}) %collective-permute-start.31) | collective-permute-done | bytes 65568 | tf_op jit(solution)/shard_map/ppermute | solution.py:150
  85.1 2.2 %collective-permute-start.32 = (f32[128,256]{1,0:T(8,128)S(1)}, f32[128,256]{1,0:T(8,128)S(1)}, u32[]{:S(2)}, u32[]{:S(2)}) collective-permute-start(f32[128,256]{1,0:T(8,128)S(1)} %weight_sum.9.half_ref), channel_id=1, source_target_pairs={{0,1},{1,0},{2,3},{3,2},{4,5},{5,4},{6,7},{7,6},{8,9},{9,8},{10,11... | collective-permute-start | bytes 393224 | tf_op jit(solution)/shard_map/ppermute | solution.py:150
  87.3 1.0 %collective-permute-done.32.other_ref = f32[128,256]{1,0:T(8,128)S(1)} collective-permute-done((f32[128,256]{1,0:T(8,128)S(1)}, f32[128,256]{1,0:T(8,128)S(1)}, u32[]{:S(2)}, u32[]{:S(2)}) %collective-permute-start.32) | collective-permute-done | bytes 131104 | tf_op jit(solution)/shard_map/ppermute | solution.py:150
  88.3 3.1 %collective-permute-done.29.q2_ref = bf16[512,256]{1,0:T(8,128)(2,1)S(1)} collective-permute-done((bf16[512,256]{1,0:T(8,128)(2,1)S(1)}, bf16[512,256]{1,0:T(8,128)(2,1)S(1)}, u32[]{:S(2)}, u32[]{:S(2)}) %collective-permute-start.29) | collective-permute-done | bytes 262176 | tf_op jit(solution)/shard_map/ppermute | solution.py:150
  91.4 0.9 finish.1
  (32 shorter events, 0.2 us)
Async XLA Ops:
  0.6 11.1 %collective-permute-start.1 = (bf16[512,256]{1,0:T(8,128)(2,1)}, bf16[512,256]{1,0:T(8,128)(2,1)S(1)}, u32[]{:S(2)}, u32[]{:S(2)}) collective-permute-start(bf16[512,256]{1,0:T(8,128)(2,1)} %source_ref.1), channel_id=1, source_target_pairs={{0,16},{8,24},{16,0},{24,8},{1,17},{9,25},{17,1},{25,9},{2,18},{10... | collective-permute-start | bytes 786440 | tf_op jit(solution)/shard_map/ppermute | solution.py:150
  0.9 10.8 %collective-permute-start = (bf16[512,256]{1,0:T(8,128)(2,1)}, bf16[512,256]{1,0:T(8,128)(2,1)S(1)}, u32[]{:S(2)}, u32[]{:S(2)}) collective-permute-start(bf16[512,256]{1,0:T(8,128)(2,1)} %source_ref.1), channel_id=1, source_target_pairs={{0,8},{8,0},{16,24},{24,16},{1,9},{9,1},{17,25},{25,17},{2,10},{10... | collective-permute-start | bytes 786440 | tf_op jit(solution)/shard_map/ppermute | solution.py:150
  2.1 12.4 %collective-permute-start.2 = (bf16[512,256]{1,0:T(8,128)(2,1)}, bf16[512,256]{1,0:T(8,128)(2,1)S(1)}, u32[]{:S(2)}, u32[]{:S(2)}) collective-permute-start(bf16[512,256]{1,0:T(8,128)(2,1)} %source_ref.1), channel_id=1, source_target_pairs={{0,24},{8,16},{16,8},{24,0},{1,25},{9,17},{17,9},{25,1},{2,26},{10... | collective-permute-start | bytes 786440 | tf_op jit(solution)/shard_map/ppermute | solution.py:150
  4.0 6.4 %copy-start.1 = (bf16[512,256]{1,0:T(8,128)(2,1)S(1)}, bf16[512,256]{1,0:T(8,128)(2,1)}, u32[]{:S(2)}) copy-start(bf16[512,256]{1,0:T(8,128)(2,1)} %source_ref.1) | copy-start | bytes 786436
  15.6 3.1 %collective-permute-start.3 = (bf16[512,256]{1,0:T(8,128)(2,1)S(1)}, bf16[512,256]{1,0:T(8,128)(2,1)S(1)}, u32[]{:S(2)}, u32[]{:S(2)}) collective-permute-start(bf16[512,256]{1,0:T(8,128)(2,1)S(1)} %get-tuple-element.36), channel_id=1, source_target_pairs={{0,1},{1,0},{2,3},{3,2},{4,5},{5,4},{6,7},{7,6},{8,9},{9,8},{10,11... | collective-permute-start | bytes 786440 | tf_op jit(solution)/shard_map/ppermute | solution.py:150
  17.5 1.5 %collective-permute-start.4 = (bf16[512,256]{1,0:T(8,128)(2,1)S(1)}, bf16[512,256]{1,0:T(8,128)(2,1)S(1)}, u32[]{:S(2)}, u32[]{:S(2)}) collective-permute-start(bf16[512,256]{1,0:T(8,128)(2,1)S(1)} %get-tuple-element.37), channel_id=1, source_target_pairs={{0,1},{1,0},{2,3},{3,2},{4,5},{5,4},{6,7},{7,6},{8,9},{9,8},{10,11... | collective-permute-start | bytes 786440 | tf_op jit(solution)/shard_map/ppermute | solution.py:150
  19.1 16.7 %collective-permute-start.13 = (bf16[512,256]{1,0:T(8,128)(2,1)S(1)}, bf16[512,256]{1,0:T(8,128)(2,1)S(1)}, u32[]{:S(2)}, u32[]{:S(2)}) collective-permute-start(bf16[512,256]{1,0:T(8,128)(2,1)S(1)} %get-tuple-element.48), channel_id=1, source_target_pairs={{0,4},{1,5},{2,6},{3,7},{4,0},{5,1},{6,2},{7,3},{8,12},{9,13},{10,... | collective-permute-start | bytes 786440 | tf_op jit(solution)/shard_map/ppermute | solution.py:150
  19.2 26.0 %collective-permute-start.14 = (bf16[512,256]{1,0:T(8,128)(2,1)S(1)}, bf16[512,256]{1,0:T(8,128)(2,1)S(1)}, u32[]{:S(2)}, u32[]{:S(2)}) collective-permute-start(bf16[512,256]{1,0:T(8,128)(2,1)S(1)} %get-tuple-element.38.refs_5_), channel_id=1, source_target_pairs={{0,6},{1,7},{2,4},{3,5},{4,2},{5,3},{6,0},{7,1},{8,14},{9,15},{10,... | collective-permute-start | bytes 786440 | tf_op jit(solution)/shard_map/ppermute | solution.py:150
  22.7 1.9 %collective-permute-start.5 = (bf16[128,256]{1,0:T(8,128)(2,1)S(1)}, bf16[128,256]{1,0:T(8,128)(2,1)S(1)}, u32[]{:S(2)}, u32[]{:S(2)}) collective-permute-start(bf16[128,256]{1,0:T(8,128)(2,1)S(1)} %get-tuple-element.39), channel_id=1, source_target_pairs={{0,1},{1,0},{2,3},{3,2},{4,5},{5,4},{6,7},{7,6},{8,9},{9,8},{10,11... | collective-permute-start | bytes 196616 | tf_op jit(solution)/shard_map/ppermute | solution.py:150
  23.7 1.3 %collective-permute-start.6 = (bf16[128,256]{1,0:T(8,128)(2,1)S(1)}, bf16[128,256]{1,0:T(8,128)(2,1)S(1)}, u32[]{:S(2)}, u32[]{:S(2)}) collective-permute-start(bf16[128,256]{1,0:T(8,128)(2,1)S(1)} %get-tuple-element.40), channel_id=1, source_target_pairs={{0,1},{1,0},{2,3},{3,2},{4,5},{5,4},{6,7},{7,6},{8,9},{9,8},{10,11... | collective-permute-start | bytes 196616 | tf_op jit(solution)/shard_map/ppermute | solution.py:150
  23.7 1.3 %collective-permute-start.7 = (bf16[128,256]{1,0:T(8,128)(2,1)S(1)}, bf16[128,256]{1,0:T(8,128)(2,1)S(1)}, u32[]{:S(2)}, u32[]{:S(2)}) collective-permute-start(bf16[128,256]{1,0:T(8,128)(2,1)S(1)} %get-tuple-element.41), channel_id=1, source_target_pairs={{0,1},{1,0},{2,3},{3,2},{4,5},{5,4},{6,7},{7,6},{8,9},{9,8},{10,11... | collective-permute-start | bytes 196616 | tf_op jit(solution)/shard_map/ppermute | solution.py:150
  24.6 1.3 %collective-permute-start.8 = (bf16[128,256]{1,0:T(8,128)(2,1)S(1)}, bf16[128,256]{1,0:T(8,128)(2,1)S(1)}, u32[]{:S(2)}, u32[]{:S(2)}) collective-permute-start(bf16[128,256]{1,0:T(8,128)(2,1)S(1)} %get-tuple-element.42), channel_id=1, source_target_pairs={{0,1},{1,0},{2,3},{3,2},{4,5},{5,4},{6,7},{7,6},{8,9},{9,8},{10,11... | collective-permute-start | bytes 196616 | tf_op jit(solution)/shard_map/ppermute | solution.py:150
  24.9 1.3 %collective-permute-start.9 = (bf16[128,256]{1,0:T(8,128)(2,1)S(1)}, bf16[128,256]{1,0:T(8,128)(2,1)S(1)}, u32[]{:S(2)}, u32[]{:S(2)}) collective-permute-start(bf16[128,256]{1,0:T(8,128)(2,1)S(1)} %get-tuple-element.43), channel_id=1, source_target_pairs={{0,1},{1,0},{2,3},{3,2},{4,5},{5,4},{6,7},{7,6},{8,9},{9,8},{10,11... | collective-permute-start | bytes 196616 | tf_op jit(solution)/shard_map/ppermute | solution.py:150
  25.1 1.3 %collective-permute-start.10 = (bf16[128,256]{1,0:T(8,128)(2,1)S(1)}, bf16[128,256]{1,0:T(8,128)(2,1)S(1)}, u32[]{:S(2)}, u32[]{:S(2)}) collective-permute-start(bf16[128,256]{1,0:T(8,128)(2,1)S(1)} %get-tuple-element.44), channel_id=1, source_target_pairs={{0,1},{1,0},{2,3},{3,2},{4,5},{5,4},{6,7},{7,6},{8,9},{9,8},{10,11... | collective-permute-start | bytes 196616 | tf_op jit(solution)/shard_map/ppermute | solution.py:150
  25.8 1.3 %collective-permute-start.11 = (bf16[128,256]{1,0:T(8,128)(2,1)S(1)}, bf16[128,256]{1,0:T(8,128)(2,1)S(1)}, u32[]{:S(2)}, u32[]{:S(2)}) collective-permute-start(bf16[128,256]{1,0:T(8,128)(2,1)S(1)} %get-tuple-element.45), channel_id=1, source_target_pairs={{0,1},{1,0},{2,3},{3,2},{4,5},{5,4},{6,7},{7,6},{8,9},{9,8},{10,11... | collective-permute-start | bytes 196616 | tf_op jit(solution)/shard_map/ppermute | solution.py:150
  26.2 1.3 %collective-permute-start.12 = (bf16[128,256]{1,0:T(8,128)(2,1)S(1)}, bf16[128,256]{1,0:T(8,128)(2,1)S(1)}, u32[]{:S(2)}, u32[]{:S(2)}) collective-permute-start(bf16[128,256]{1,0:T(8,128)(2,1)S(1)} %get-tuple-element.46), channel_id=1, source_target_pairs={{0,1},{1,0},{2,3},{3,2},{4,5},{5,4},{6,7},{7,6},{8,9},{9,8},{10,11... | collective-permute-start | bytes 196616 | tf_op jit(solution)/shard_map/ppermute | solution.py:150
  28.4 16.9 %collective-permute-start.15 = (bf16[256,256]{1,0:T(8,128)(2,1)S(1)}, bf16[256,256]{1,0:T(8,128)(2,1)S(1)}, u32[]{:S(2)}, u32[]{:S(2)}) collective-permute-start(bf16[256,256]{1,0:T(8,128)(2,1)S(1)} %get-tuple-element.49), channel_id=1, source_target_pairs={{0,2},{1,3},{2,0},{3,1},{4,6},{5,7},{6,4},{7,5},{8,10},{9,11},{10,... | collective-permute-start | bytes 393224 | tf_op jit(solution)/shard_map/ppermute | solution.py:150
  29.5 15.8 %copy-start = (bf16[512,256]{1,0:T(8,128)(2,1)S(1)}, bf16[512,256]{1,0:T(8,128)(2,1)}, u32[]{:S(2)}) copy-start(bf16[512,256]{1,0:T(8,128)(2,1)} %cotangent_ref.1) | copy-start | bytes 786436
  29.5 15.8 %copy-start.2 = (bf16[256,256]{1,0:T(8,128)(2,1)S(1)}, bf16[256,256]{1,0:T(8,128)(2,1)}, u32[]{:S(2)}) copy-start(bf16[256,256]{1,0:T(8,128)(2,1)} %weight_ref.1) | copy-start | bytes 393220
  29.5 15.7 %collective-permute-start.16 = (bf16[256,256]{1,0:T(8,128)(2,1)S(1)}, bf16[256,256]{1,0:T(8,128)(2,1)S(1)}, u32[]{:S(2)}, u32[]{:S(2)}) collective-permute-start(bf16[256,256]{1,0:T(8,128)(2,1)S(1)} %get-tuple-element.50), channel_id=1, source_target_pairs={{0,2},{1,3},{2,0},{3,1},{4,6},{5,7},{6,4},{7,5},{8,10},{9,11},{10,... | collective-permute-start | bytes 393224 | tf_op jit(solution)/shard_map/ppermute | solution.py:150
  46.4 14.3 %collective-permute-start.18 = (bf16[512,256]{1,0:T(8,128)(2,1)S(1)}, bf16[512,256]{1,0:T(8,128)(2,1)S(1)}, u32[]{:S(2)}, u32[]{:S(2)}) collective-permute-start(bf16[512,256]{1,0:T(8,128)(2,1)S(1)} %get-tuple-element.52.refs_0_), channel_id=1, source_target_pairs={{0,2},{1,3},{2,0},{3,1},{4,6},{5,7},{6,4},{7,5},{8,10},{9,11},{10,... | collective-permute-start | bytes 786440 | tf_op jit(solution)/shard_map/ppermute | solution.py:150
  47.5 15.6 %collective-permute-start.17 = (bf16[512,256]{1,0:T(8,128)(2,1)S(1)}, bf16[512,256]{1,0:T(8,128)(2,1)S(1)}, u32[]{:S(2)}, u32[]{:S(2)}) collective-permute-start(bf16[512,256]{1,0:T(8,128)(2,1)S(1)} %get-tuple-element.52.refs_0_), channel_id=1, source_target_pairs={{0,1},{1,0},{2,3},{3,2},{4,5},{5,4},{6,7},{7,6},{8,9},{9,8},{10,11... | collective-permute-start | bytes 786440 | tf_op jit(solution)/shard_map/ppermute | solution.py:150
  48.2 16.7 %collective-permute-start.21 = (bf16[512,256]{1,0:T(8,128)(2,1)S(1)}, bf16[512,256]{1,0:T(8,128)(2,1)S(1)}, u32[]{:S(2)}, u32[]{:S(2)}) collective-permute-start(bf16[512,256]{1,0:T(8,128)(2,1)S(1)} %get-tuple-element.52.refs_0_), channel_id=1, source_target_pairs={{0,4},{1,5},{2,6},{3,7},{4,0},{5,1},{6,2},{7,3},{8,12},{9,13},{10,... | collective-permute-start | bytes 786440 | tf_op jit(solution)/shard_map/ppermute | solution.py:150
  48.2 25.0 %collective-permute-start.20 = (bf16[512,256]{1,0:T(8,128)(2,1)S(1)}, bf16[512,256]{1,0:T(8,128)(2,1)S(1)}, u32[]{:S(2)}, u32[]{:S(2)}) collective-permute-start(bf16[512,256]{1,0:T(8,128)(2,1)S(1)} %get-tuple-element.52.refs_0_), channel_id=1, source_target_pairs={{0,6},{1,7},{2,4},{3,5},{4,2},{5,3},{6,0},{7,1},{8,14},{9,15},{10,... | collective-permute-start | bytes 786440 | tf_op jit(solution)/shard_map/ppermute | solution.py:150
  50.1 1.5 %collective-permute-start.22 = (bf16[128,256]{1,0:T(8,128)(2,1)S(1)}, bf16[128,256]{1,0:T(8,128)(2,1)S(1)}, u32[]{:S(2)}, u32[]{:S(2)}) collective-permute-start(bf16[128,256]{1,0:T(8,128)(2,1)S(1)} %get-tuple-element.58), channel_id=1, source_target_pairs={{0,1},{1,0},{2,3},{3,2},{4,5},{5,4},{6,7},{7,6},{8,9},{9,8},{10,11... | collective-permute-start | bytes 196616 | tf_op jit(solution)/shard_map/ppermute | solution.py:150
  51.7 3.5 %collective-permute-start.23 = (bf16[128,256]{1,0:T(8,128)(2,1)S(1)}, bf16[128,256]{1,0:T(8,128)(2,1)S(1)}, u32[]{:S(2)}, u32[]{:S(2)}) collective-permute-start(bf16[128,256]{1,0:T(8,128)(2,1)S(1)} %weight_sum.5.mine_ref), channel_id=1, source_target_pairs={{0,8},{8,0},{16,24},{24,16},{1,9},{9,1},{17,25},{25,17},{2,10},{10... | collective-permute-start | bytes 196616 | tf_op jit(solution)/shard_map/ppermute | solution.py:150
  55.2 3.5 %collective-permute-start.24 = (bf16[128,256]{1,0:T(8,128)(2,1)S(1)}, bf16[128,256]{1,0:T(8,128)(2,1)S(1)}, u32[]{:S(2)}, u32[]{:S(2)}) collective-permute-start(bf16[128,256]{1,0:T(8,128)(2,1)S(1)} %weight_sum.6.mine_ref), channel_id=1, source_target_pairs={{0,16},{8,24},{16,0},{24,8},{1,17},{9,25},{17,1},{25,9},{2,18},{10... | collective-permute-start | bytes 196616 | tf_op jit(solution)/shard_map/ppermute | solution.py:150
  58.7 14.6 %collective-permute-start.25 = (bf16[128,256]{1,0:T(8,128)(2,1)S(1)}, bf16[128,256]{1,0:T(8,128)(2,1)S(1)}, u32[]{:S(2)}, u32[]{:S(2)}) collective-permute-start(bf16[128,256]{1,0:T(8,128)(2,1)S(1)} %weight_sum.7.mine_ref), channel_id=1, source_target_pairs={{0,2},{1,3},{2,0},{3,1},{4,6},{5,7},{6,4},{7,5},{8,10},{9,11},{10,... | collective-permute-start | bytes 196616 | tf_op jit(solution)/shard_map/ppermute | solution.py:150
  60.7 13.5 %collective-permute-start.19 = (bf16[512,256]{1,0:T(8,128)(2,1)S(1)}, bf16[512,256]{1,0:T(8,128)(2,1)S(1)}, u32[]{:S(2)}, u32[]{:S(2)}) collective-permute-start(bf16[512,256]{1,0:T(8,128)(2,1)S(1)} %collective-permute-done.18.refs_2_), channel_id=1, source_target_pairs={{0,1},{1,0},{2,3},{3,2},{4,5},{5,4},{6,7},{7,6},{8,9},{9,8},{10,11... | collective-permute-start | bytes 786440 | tf_op jit(solution)/shard_map/ppermute | solution.py:150
  73.3 2.8 %collective-permute-start.26 = (bf16[512,256]{1,0:T(8,128)(2,1)S(1)}, bf16[512,256]{1,0:T(8,128)(2,1)S(1)}, u32[]{:S(2)}, u32[]{:S(2)}) collective-permute-start(bf16[512,256]{1,0:T(8,128)(2,1)S(1)} %get-tuple-element.59.refs_1_), channel_id=1, source_target_pairs={{0,1},{1,0},{2,3},{3,2},{4,5},{5,4},{6,7},{7,6},{8,9},{9,8},{10,11... | collective-permute-start | bytes 786440 | tf_op jit(solution)/shard_map/ppermute | solution.py:150
  74.1 2.0 %collective-permute-start.27 = (bf16[512,256]{1,0:T(8,128)(2,1)S(1)}, bf16[512,256]{1,0:T(8,128)(2,1)S(1)}, u32[]{:S(2)}, u32[]{:S(2)}) collective-permute-start(bf16[512,256]{1,0:T(8,128)(2,1)S(1)} %get-tuple-element.60.refs_2_), channel_id=1, source_target_pairs={{0,1},{1,0},{2,3},{3,2},{4,5},{5,4},{6,7},{7,6},{8,9},{9,8},{10,11... | collective-permute-start | bytes 786440 | tf_op jit(solution)/shard_map/ppermute | solution.py:150
  76.6 11.7 %collective-permute-start.28 = (bf16[512,256]{1,0:T(8,128)(2,1)S(1)}, bf16[512,256]{1,0:T(8,128)(2,1)S(1)}, u32[]{:S(2)}, u32[]{:S(2)}) collective-permute-start(bf16[512,256]{1,0:T(8,128)(2,1)S(1)} %backward_far_away.2.refs_4_), channel_id=1, source_target_pairs={{0,24},{8,16},{16,8},{24,0},{1,25},{9,17},{17,9},{25,1},{2,26},{10... | collective-permute-start | bytes 786440 | tf_op jit(solution)/shard_map/ppermute | solution.py:150
  78.6 12.8 %collective-permute-start.29 = (bf16[512,256]{1,0:T(8,128)(2,1)S(1)}, bf16[512,256]{1,0:T(8,128)(2,1)S(1)}, u32[]{:S(2)}, u32[]{:S(2)}) collective-permute-start(bf16[512,256]{1,0:T(8,128)(2,1)S(1)} %get-tuple-element.61), channel_id=1, source_target_pairs={{0,16},{8,24},{16,0},{24,8},{1,17},{9,25},{17,1},{25,9},{2,18},{10... | collective-permute-start | bytes 786440 | tf_op jit(solution)/shard_map/ppermute | solution.py:150
  79.9 11.5 %collective-permute-start.30 = (bf16[512,256]{1,0:T(8,128)(2,1)S(1)}, bf16[512,256]{1,0:T(8,128)(2,1)S(1)}, u32[]{:S(2)}, u32[]{:S(2)}) collective-permute-start(bf16[512,256]{1,0:T(8,128)(2,1)S(1)} %get-tuple-element.62), channel_id=1, source_target_pairs={{0,8},{8,0},{16,24},{24,16},{1,9},{9,1},{17,25},{25,17},{2,10},{10... | collective-permute-start | bytes 786440 | tf_op jit(solution)/shard_map/ppermute | solution.py:150
  80.7 4.4 %collective-permute-start.31 = (bf16[128,256]{1,0:T(8,128)(2,1)S(1)}, bf16[128,256]{1,0:T(8,128)(2,1)S(1)}, u32[]{:S(2)}, u32[]{:S(2)}) collective-permute-start(bf16[128,256]{1,0:T(8,128)(2,1)S(1)} %later.5.mine_ref), channel_id=1, source_target_pairs={{0,4},{1,5},{2,6},{3,7},{4,0},{5,1},{6,2},{7,3},{8,12},{9,13},{10,... | collective-permute-start | bytes 196616 | tf_op jit(solution)/shard_map/ppermute | solution.py:150
  85.1 3.2 %collective-permute-start.32 = (f32[128,256]{1,0:T(8,128)S(1)}, f32[128,256]{1,0:T(8,128)S(1)}, u32[]{:S(2)}, u32[]{:S(2)}) collective-permute-start(f32[128,256]{1,0:T(8,128)S(1)} %weight_sum.9.half_ref), channel_id=1, source_target_pairs={{0,1},{1,0},{2,3},{3,2},{4,5},{5,4},{6,7},{7,6},{8,9},{9,8},{10,11... | collective-permute-start | bytes 393224 | tf_op jit(solution)/shard_map/ppermute | solution.py:150

commit v3 on v2

--- a/solution.py
+++ b/solution.py
@@ -242,14 +242,13 @@
 
 
 def middle_kernel(weight_ref, cotangent_ref, mine_ref, far_ref, *refs):
-    *near_refs, activated_ref, sent_ref, mixed_ref, slope_ref = refs
+    *near_refs, sent_ref, mixed_ref, slope_ref = refs
     near = jnp.concatenate([ref[...] for ref in near_refs], axis=0)
     mixed = mine_ref[...] + near.astype(F32) + far_ref[...]
     mixed = mixed.astype(BF16)
     weight = weight_ref[...]
     summed = jnp.dot(mixed, weight, preferred_element_type=F32)
     sigma = 1.0 / (1.0 + jnp.exp(-summed))
-    activated_ref[...] = (summed * sigma).astype(BF16)
     slope = cotangent_ref[...].astype(F32) * sigma * (1.0 + summed * (1.0 - sigma))
     slope = slope.astype(BF16)
     sent_ref[...] = lax.dot_general(
@@ -259,10 +258,12 @@
     slope_ref[...] = slope
 
 
-def term_kernel(mixed_ref, slope_ref, keep_ref, send_ref, term_ref):
+def term_kernel(mixed_ref, slope_ref, weight_ref, keep_ref, send_ref, activated_ref, term_ref):
     term_ref[...] = lax.dot_general(
         mixed_ref[...], slope_ref[...], (((0,), (0,)), ((), ())), preferred_element_type=F32
     )
+    summed = jnp.dot(mixed_ref[...], weight_ref[...], preferred_element_type=F32)
+    activated_ref[...] = (summed / (1.0 + jnp.exp(-summed))).astype(BF16)
     half = keep_ref.shape[0]
     core = lax.axis_index("col") % 2
     keep_ref[...] = term_ref[pl.ds(pl.multiple_of(core * half, half), half), :]
@@ -303,13 +304,16 @@
         out_ref[...] = total.astype(out_ref.dtype)
 
 
-def finish_kernel(mine_ref, q1_ref, q2_ref, q3_ref, half_ref, other_ref, nodes_ref, weight_ref):
+def total_kernel(mine_ref, q1_ref, q2_ref, q3_ref, out_ref):
     total = mine_ref[...] + q1_ref[...].astype(F32) + q2_ref[...].astype(F32) + q3_ref[...].astype(F32)
-    nodes_ref[...] = total.astype(nodes_ref.dtype)
+    out_ref[...] = total.astype(out_ref.dtype)
+
+
+def halves_kernel(half_ref, other_ref, out_ref):
     half = half_ref.shape[0]
     core = lax.axis_index("col") % 2
-    weight_ref[pl.ds(pl.multiple_of(core * half, half), half), :] = half_ref[...]
-    weight_ref[pl.ds(pl.multiple_of((1 - core) * half, half), half), :] = other_ref[...]
+    out_ref[pl.ds(pl.multiple_of(core * half, half), half), :] = half_ref[...]
+    out_ref[pl.ds(pl.multiple_of((1 - core) * half, half), half), :] = other_ref[...]
 
 
 def sum_kernel(mine_ref, other_ref, out_ref):
@@ -373,8 +377,8 @@
     )
     near = [swap(value, "col", 2) for value in near]
     joined = kernel_call(join_kernel, exact, (r2, r3), "join_far", flops=COVER)
-    activated, sent, mixed, slope = kernel_call(
-        middle_kernel, [block] * 4, (weight, cotangent, held(mine), held(joined), *near), "middle"
+    sent, mixed, slope = kernel_call(
+        middle_kernel, [block] * 3, (weight, cotangent, held(mine), held(joined), *near), "middle"
     )
     s3, s2, s1 = (swap(sent, "col", 2 * d) for d in (3, 2, 1))
     o0, o1 = swap(sent, "col", 1), swap(s1, "col", 1)
@@ -384,8 +388,8 @@
         return kernel_call(sum_kernel, out_shape, (value, swap(value, axis, distance)), "weight_sum", after=after)
 
     short = jax.ShapeDtypeStruct(half.shape, BF16)
-    keep, send = kernel_call(
-        term_kernel, [half, short], (mixed, slope), "weight_term", scratch=(pltpu.VMEM(whole.shape, F32),)
+    keep, send, activated = kernel_call(
+        term_kernel, [half, short, block], (mixed, slope, weight), "weight_term", scratch=(pltpu.VMEM(whole.shape, F32),)
     )
     term = kernel_call(sum_kernel, short, (keep, swap(send, "col", 1)), "weight_sum")
     term = add(term, "row", 1, BF16)
@@ -414,9 +418,8 @@
         (adjacency, held(start), o2, o3), "backward_mine", after=(shares[0],),
     )[0]
     term = add(later((term,), (mine,))[0], "col", 4, F32)
-    grad_features, grad_weight = kernel_call(
-        finish_kernel, [block, whole], (held(mine), *returned, term, swap(term, "col", 1)), "finish"
-    )
+    grad_weight = kernel_call(halves_kernel, whole, (term, swap(term, "col", 1)), "weight_halves")
+    grad_features = kernel_call(total_kernel, block, (held(mine), *returned), "total")
     return (activated, grad_features, grad_weight)
 
 

time: 92.5 us -> 91.9 us (level)
  the two profiles are of different devices: /device:TPU:21 before, /device:TPU:0 now
where the time goes in v3:
time: 91.9 us; the launch traced here: 90.1 us
  waiting for transfers between devices  34.5 us (38%)
  starting transfers between devices  32.2 us (35%)
  Pallas kernels  22 us (24%)
  between operations  1.52 us (2%)
    ppermute x33, waiting for transfers between devices, swap(): return lax.ppermute(value, axis, [(i, i ^ distance) for i in range(count)])  34.5 us
    ppermute x33, starting transfers between devices, swap(): return lax.ppermute(value, axis, [(i, i ^ distance) for i in range(count)])  32.2 us
    pallas_call x22, Pallas kernels, kernel_call(): pl.pallas_call(ordered if after else kernel, out_shape=out_shape, in_spec...  22 us
  transfers between devices with their start and end apart: 33, of which 16 were waited for; matrix products, arithmetic and copies ran while one was open for 0% of the time, Pallas kernels for 21%

profile of v3, /device:TPU:0, one launch (start us, length us, event | category | flops | bytes accessed | tf_op | source)
XLA Modules:
  0.0 90.1 jit_solution(16611067196352744095)
XLA Ops:
  0.6 3.0 %collective-permute-start.1 = (bf16[512,256]{1,0:T(8,128)(2,1)}, bf16[512,256]{1,0:T(8,128)(2,1)S(1)}, u32[]{:S(2)}, u32[]{:S(2)}) collective-permute-start(bf16[512,256]{1,0:T(8,128)(2,1)} %source_ref.1), channel_id=1, source_target_pairs={{0,16},{8,24},{16,0},{24,8},{1,17},{9,25},{17,1},{25,9},{2,18},{10... | collective-permute-start | bytes 786440 | tf_op jit(solution)/shard_map/ppermute | solution.py:150
  3.7 1.5 %collective-permute-start = (bf16[512,256]{1,0:T(8,128)(2,1)}, bf16[512,256]{1,0:T(8,128)(2,1)S(1)}, u32[]{:S(2)}, u32[]{:S(2)}) collective-permute-start(bf16[512,256]{1,0:T(8,128)(2,1)} %source_ref.1), channel_id=1, source_target_pairs={{0,8},{8,0},{16,24},{24,16},{1,9},{9,1},{17,25},{25,17},{2,10},{10... | collective-permute-start | bytes 786440 | tf_op jit(solution)/shard_map/ppermute | solution.py:150
  5.2 0.0 collective-permute-start.2
  5.9 7.9 %load_tiles.1.adjacency_ref.refs_0_ = bf16[4096,2048]{1,0:T(8,128)(2,1)S(1)} custom-call(s32[1,1]{1,0:T(1,128)S(6)} %copy.20.count_ref, s32[512]{0:T(512)} %row_ref.1, s32[512]{0:T(512)} %col_ref.1, bf16[512,128,128]{2,1,0:T(8,128)(2,1)} %tiles_ref.1), custom_call_target="tpu_custom_call" | custom-call | tf_op jit(solution)/shard_map/load_tiles/pallas_call | solution.py:119
  13.8 1.3 %forward_own.1.refs_3_.refs_4_ = f32[4096,256]{1,0:T(8,128)S(1)} custom-call(bf16[4096,2048]{1,0:T(8,128)(2,1)S(1)} %load_tiles.1.adjacency_ref.refs_0_, bf16[512,256]{1,0:T(8,128)(2,1)S(1)} %copy-done.2), custom_call_target="tpu_custom_call" | custom-call | tf_op jit(solution)/shard_map/forward_own/pallas_call | solution.py:119
  15.1 2.0 %collective-permute-done.2.refs_2_.refs_3_ = bf16[512,256]{1,0:T(8,128)(2,1)S(1)} collective-permute-done((bf16[512,256]{1,0:T(8,128)(2,1)}, bf16[512,256]{1,0:T(8,128)(2,1)S(1)}, u32[]{:S(2)}, u32[]{:S(2)}) %collective-permute-start.2) | collective-permute-done | bytes 262176 | tf_op jit(solution)/shard_map/ppermute | solution.py:150
  17.1 1.0 %forward_away_far.1 = (bf16[512,256]{1,0:T(8,128)(2,1)S(1)}, bf16[512,256]{1,0:T(8,128)(2,1)S(1)}) custom-call(bf16[4096,2048]{1,0:T(8,128)(2,1)S(1)} %load_tiles.1.adjacency_ref.refs_0_, bf16[512,256]{1,0:T(8,128)(2,1)S(1)} %collective-permute-done.refs_0_.refs_1_, bf16[512,256]{1,0:T(8,128)(2,1)S(1)} %collective-permute-done.1.refs_1_.refs_2_, ...), custom_call_target="tpu_custom_call" | custom-call | tf_op jit(solution)/shard_map/forward_away_far/pallas_call | solution.py:119
  18.0 0.1 collective-permute-start.3
  18.1 0.5 collective-permute-start.4
  18.6 1.0 %forward_home_far.1 = (f32[512,256]{1,0:T(8,128)S(1)}, f32[512,256]{1,0:T(8,128)S(1)}) custom-call(bf16[4096,2048]{1,0:T(8,128)(2,1)S(1)} %load_tiles.1.adjacency_ref.refs_0_, bf16[512,256]{1,0:T(8,128)(2,1)S(1)} %collective-permute-done.refs_0_.refs_1_, bf16[512,256]{1,0:T(8,128)(2,1)S(1)} %collective-permute-done.1.refs_1_.refs_2_, ...), custom_call_target="tpu_custom_call" | custom-call | tf_op jit(solution)/shard_map/forward_home_far/pallas_call | solution.py:119
  19.6 0.4 collective-permute-done.4.refs_3_
  20.0 0.1 add_far.1
  20.1 2.8 %collective-permute-start.13 = (bf16[512,256]{1,0:T(8,128)(2,1)S(1)}, bf16[512,256]{1,0:T(8,128)(2,1)S(1)}, u32[]{:S(2)}, u32[]{:S(2)}) collective-permute-start(bf16[512,256]{1,0:T(8,128)(2,1)S(1)} %get-tuple-element.46), channel_id=1, source_target_pairs={{0,4},{1,5},{2,6},{3,7},{4,0},{5,1},{6,2},{7,3},{8,12},{9,13},{10,... | collective-permute-start | bytes 786440 | tf_op jit(solution)/shard_map/ppermute | solution.py:150
  22.9 1.3 %collective-permute-start.14 = (bf16[512,256]{1,0:T(8,128)(2,1)S(1)}, bf16[512,256]{1,0:T(8,128)(2,1)S(1)}, u32[]{:S(2)}, u32[]{:S(2)}) collective-permute-start(bf16[512,256]{1,0:T(8,128)(2,1)S(1)} %get-tuple-element.36.refs_5_), channel_id=1, source_target_pairs={{0,6},{1,7},{2,4},{3,5},{4,2},{5,3},{6,0},{7,1},{8,14},{9,15},{10,... | collective-permute-start | bytes 786440 | tf_op jit(solution)/shard_map/ppermute | solution.py:150
  24.3 1.0 %forward_away_near.1 = (bf16[128,256]{1,0:T(8,128)(2,1)S(1)}, bf16[128,256]{1,0:T(8,128)(2,1)S(1)}, bf16[128,256]{1,0:T(8,128)(2,1)S(1)}, bf16[128,256]{1,0:T(8,...) custom-call(bf16[4096,2048]{1,0:T(8,128)(2,1)S(1)} %load_tiles.1.adj, ...), custom_call_target="tpu_custom_call" | custom-call | tf_op jit(solution)/shard_map/forward_away_near/pallas_call | solution.py:119
  25.3 0.1 collective-permute-start.5
  25.3 0.5 collective-permute-start.6
  25.8 0.1 collective-permute-start.7
  25.9 0.7 collective-permute-done.5.refs_4_
  26.6 0.2 collective-permute-start.8
  26.7 0.4 collective-permute-start.9
  27.1 0.2 collective-permute-start.10
  27.3 0.6 collective-permute-done.8.refs_7_
  27.8 0.2 collective-permute-start.11
  28.0 0.4 collective-permute-start.12
  28.4 0.7 collective-permute-done.11.refs_10_
  29.1 0.2 collective-permute-done.12.refs_11_
  29.3 1.0 %forward_home_near.1 = (bf16[256,256]{1,0:T(8,128)(2,1)S(1)}, bf16[256,256]{1,0:T(8,128)(2,1)S(1)}, f32[512,256]{1,0:T(8,128)S(1)}) custom-call(bf16[4096,2048]{1,0:T(8,128)(2,1)S(1)} %load_tiles.1.adjacency_ref.refs_0_, bf16[512,256]{1,0:T(8,128)(2,1)S(1)} %collective-permute-done.refs_0_.refs_1_, ...), custom_call_target="tpu_custom_call" | custom-call | tf_op jit(solution)/shard_map/forward_home_near/pallas_call | solution.py:119
  30.2 0.3 collective-permute-start.15
  30.5 1.8 %collective-permute-start.16 = (bf16[256,256]{1,0:T(8,128)(2,1)S(1)}, bf16[256,256]{1,0:T(8,128)(2,1)S(1)}, u32[]{:S(2)}, u32[]{:S(2)}) collective-permute-start(bf16[256,256]{1,0:T(8,128)(2,1)S(1)} %get-tuple-element.48), channel_id=1, source_target_pairs={{0,2},{1,3},{2,0},{3,1},{4,6},{5,7},{6,4},{7,5},{8,10},{9,11},{10,... | collective-permute-start | bytes 393224 | tf_op jit(solution)/shard_map/ppermute | solution.py:150
  32.3 9.2 %collective-permute-done.13.a_ref = bf16[512,256]{1,0:T(8,128)(2,1)S(1)} collective-permute-done((bf16[512,256]{1,0:T(8,128)(2,1)S(1)}, bf16[512,256]{1,0:T(8,128)(2,1)S(1)}, u32[]{:S(2)}, u32[]{:S(2)}) %collective-permute-start.13) | collective-permute-done | bytes 262176 | tf_op jit(solution)/shard_map/ppermute | solution.py:150
  41.5 0.1 join_far.1.far_ref
  41.6 2.1 %collective-permute-done.15.refs_0_ = bf16[256,256]{1,0:T(8,128)(2,1)S(1)} collective-permute-done((bf16[256,256]{1,0:T(8,128)(2,1)S(1)}, bf16[256,256]{1,0:T(8,128)(2,1)S(1)}, u32[]{:S(2)}, u32[]{:S(2)}) %collective-permute-start.15) | collective-permute-done | bytes 131104 | tf_op jit(solution)/shard_map/ppermute | solution.py:150
  43.6 2.8 %collective-permute-done.16.refs_1_ = bf16[256,256]{1,0:T(8,128)(2,1)S(1)} collective-permute-done((bf16[256,256]{1,0:T(8,128)(2,1)S(1)}, bf16[256,256]{1,0:T(8,128)(2,1)S(1)}, u32[]{:S(2)}, u32[]{:S(2)}) %collective-permute-start.16) | collective-permute-done | bytes 131104 | tf_op jit(solution)/shard_map/ppermute | solution.py:150
  46.4 0.5 middle.1
  46.9 0.9 %collective-permute-start.18 = (bf16[512,256]{1,0:T(8,128)(2,1)S(1)}, bf16[512,256]{1,0:T(8,128)(2,1)S(1)}, u32[]{:S(2)}, u32[]{:S(2)}) collective-permute-start(bf16[512,256]{1,0:T(8,128)(2,1)S(1)} %get-tuple-element.52.refs_0_), channel_id=1, source_target_pairs={{0,2},{1,3},{2,0},{3,1},{4,6},{5,7},{6,4},{7,5},{8,10},{9,11},{10,... | collective-permute-start | bytes 786440 | tf_op jit(solution)/shard_map/ppermute | solution.py:150
  47.8 3.2 %collective-permute-start.21 = (bf16[512,256]{1,0:T(8,128)(2,1)S(1)}, bf16[512,256]{1,0:T(8,128)(2,1)S(1)}, u32[]{:S(2)}, u32[]{:S(2)}) collective-permute-start(bf16[512,256]{1,0:T(8,128)(2,1)S(1)} %get-tuple-element.52.refs_0_), channel_id=1, source_target_pairs={{0,4},{1,5},{2,6},{3,7},{4,0},{5,1},{6,2},{7,3},{8,12},{9,13},{10,... | collective-permute-start | bytes 786440 | tf_op jit(solution)/shard_map/ppermute | solution.py:150
  51.0 0.3 collective-permute-start.20
  51.3 1.0 %weight_term.1 = (f32[128,256]{1,0:T(8,128)S(1)}, bf16[128,256]{1,0:T(8,128)(2,1)S(1)}, bf16[512,256]{1,0:T(8,128)(2,1)}) custom-call(bf16[512,256]{1,0:T(8,128)(2,1)S(1)} %get-tuple-element.49.mixed_ref, bf16[512,256]{1,0:T(8,128)(2,1)S(1)} %get-tuple-element.50.slope_ref, bf16[256,256]{1,0:T(8,128)(2,1)S(1)} %copy-done), custom_call_target="tpu_custom_call" | custom-call | tf_op jit(solution)/shard_map/weight_term/pallas_call | solution.py:119
  52.4 0.1 collective-permute-start.22
  52.4 1.2 %collective-permute-done.22.other_ref = bf16[128,256]{1,0:T(8,128)(2,1)S(1)} collective-permute-done((bf16[128,256]{1,0:T(8,128)(2,1)S(1)}, bf16[128,256]{1,0:T(8,128)(2,1)S(1)}, u32[]{:S(2)}, u32[]{:S(2)}) %collective-permute-start.22) | collective-permute-done | bytes 65568 | tf_op jit(solution)/shard_map/ppermute | solution.py:150
  53.6 1.6 %collective-permute-start.23 = (bf16[128,256]{1,0:T(8,128)(2,1)S(1)}, bf16[128,256]{1,0:T(8,128)(2,1)S(1)}, u32[]{:S(2)}, u32[]{:S(2)}) collective-permute-start(bf16[128,256]{1,0:T(8,128)(2,1)S(1)} %weight_sum.5.mine_ref), channel_id=1, source_target_pairs={{0,8},{8,0},{16,24},{24,16},{1,9},{9,1},{17,25},{25,17},{2,10},{10... | collective-permute-start | bytes 196616 | tf_op jit(solution)/shard_map/ppermute | solution.py:150
  55.2 2.7 %collective-permute-done.23.other_ref = bf16[128,256]{1,0:T(8,128)(2,1)S(1)} collective-permute-done((bf16[128,256]{1,0:T(8,128)(2,1)S(1)}, bf16[128,256]{1,0:T(8,128)(2,1)S(1)}, u32[]{:S(2)}, u32[]{:S(2)}) %collective-permute-start.23) | collective-permute-done | bytes 65568 | tf_op jit(solution)/shard_map/ppermute | solution.py:150
  58.0 1.6 %collective-permute-start.24 = (bf16[128,256]{1,0:T(8,128)(2,1)S(1)}, bf16[128,256]{1,0:T(8,128)(2,1)S(1)}, u32[]{:S(2)}, u32[]{:S(2)}) collective-permute-start(bf16[128,256]{1,0:T(8,128)(2,1)S(1)} %weight_sum.6.mine_ref), channel_id=1, source_target_pairs={{0,16},{8,24},{16,0},{24,8},{1,17},{9,25},{17,1},{25,9},{2,18},{10... | collective-permute-start | bytes 196616 | tf_op jit(solution)/shard_map/ppermute | solution.py:150
  59.6 2.7 %collective-permute-done.24.other_ref = bf16[128,256]{1,0:T(8,128)(2,1)S(1)} collective-permute-done((bf16[128,256]{1,0:T(8,128)(2,1)S(1)}, bf16[128,256]{1,0:T(8,128)(2,1)S(1)}, u32[]{:S(2)}, u32[]{:S(2)}) %collective-permute-start.24) | collective-permute-done | bytes 65568 | tf_op jit(solution)/shard_map/ppermute | solution.py:150
  62.4 0.5 collective-permute-start.25
  62.8 1.9 %backward_home.1.refs_2_.start_ref = f32[2048,256]{1,0:T(8,128)S(1)} custom-call(bf16[4096,2048]{1,0:T(8,128)(2,1)S(1)} %load_tiles.1.adjacency_ref.refs_0_, bf16[512,256]{1,0:T(8,128)(2,1)S(1)} %get-tuple-element.52.refs_0_, bf16[512,256]{1,0:T(8,128)(2,1)S(1)} %collective-permute-done.17.refs_1_, bf16[512,256]{1,0:T(8,128)(2,1)S(1)} %collective-permute-done.18.refs_2_), custom_call_target="tpu_custom_call" | custom-call | tf_op jit(solution)/shard_map/backward_home/pallas_call | solution.py:119
  64.7 4.8 %collective-permute-done.21.refs_1_ = bf16[512,256]{1,0:T(8,128)(2,1)S(1)} collective-permute-done((bf16[512,256]{1,0:T(8,128)(2,1)S(1)}, bf16[512,256]{1,0:T(8,128)(2,1)S(1)}, u32[]{:S(2)}, u32[]{:S(2)}) %collective-permute-start.21) | collective-permute-done | bytes 262176 | tf_op jit(solution)/shard_map/ppermute | solution.py:150
  69.5 0.9 collective-permute-done.25.other_ref
  70.4 0.1 collective-permute-start.26
  70.5 0.5 collective-permute-start.27
  71.0 1.9 %backward_most.1.start_ref.refs_1_ = f32[2048,256]{1,0:T(8,128)S(1)} custom-call(bf16[4096,2048]{1,0:T(8,128)(2,1)S(1)} %load_tiles.1.adjacency_ref.refs_0_, f32[2048,256]{1,0:T(8,128)S(1)} %backward_home.1.refs_2_.start_ref, bf16[512,256]{1,0:T(8,128)(2,1)S(1)} %collective-permute-done.19.refs_0_, bf16[512,256]{1,0:T(8,128)(2,1)S(1)} %get-tuple-element.57.refs_1_, ...), custom_call_target="tpu_custom_call" | custom-call | tf_op jit(solution)/shard_map/backward_most/pallas_call | solution.py:119
  72.9 0.5 backward_far_away.2.refs_4_
  73.4 2.5 %collective-permute-start.28 = (bf16[512,256]{1,0:T(8,128)(2,1)S(1)}, bf16[512,256]{1,0:T(8,128)(2,1)S(1)}, u32[]{:S(2)}, u32[]{:S(2)}) collective-permute-start(bf16[512,256]{1,0:T(8,128)(2,1)S(1)} %backward_far_away.2.refs_4_), channel_id=1, source_target_pairs={{0,24},{8,16},{16,8},{24,0},{1,25},{9,17},{17,9},{25,1},{2,26},{10... | collective-permute-start | bytes 786440 | tf_op jit(solution)/shard_map/ppermute | solution.py:150
  76.0 0.8 backward_far_away.3
  76.8 0.6 collective-permute-start.29
  77.3 0.5 collective-permute-start.30
  77.8 0.5 backward_mine.1.mine_ref.refs_1_
  78.4 6.5 %collective-permute-start.31 = (bf16[128,256]{1,0:T(8,128)(2,1)S(1)}, bf16[128,256]{1,0:T(8,128)(2,1)S(1)}, u32[]{:S(2)}, u32[]{:S(2)}) collective-permute-start(bf16[128,256]{1,0:T(8,128)(2,1)S(1)} %later.5.mine_ref), channel_id=1, source_target_pairs={{0,4},{1,5},{2,6},{3,7},{4,0},{5,1},{6,2},{7,3},{8,12},{9,13},{10,... | collective-permute-start | bytes 196616 | tf_op jit(solution)/shard_map/ppermute | solution.py:150
  84.9 2.3 %collective-permute-done.31.other_ref = bf16[128,256]{1,0:T(8,128)(2,1)S(1)} collective-permute-done((bf16[128,256]{1,0:T(8,128)(2,1)S(1)}, bf16[128,256]{1,0:T(8,128)(2,1)S(1)}, u32[]{:S(2)}, u32[]{:S(2)}) %collective-permute-start.31) | collective-permute-done | bytes 65568 | tf_op jit(solution)/shard_map/ppermute | solution.py:150
  87.1 0.1 collective-permute-start.32
  87.2 1.3 %collective-permute-done.32.other_ref = f32[128,256]{1,0:T(8,128)S(1)} collective-permute-done((f32[128,256]{1,0:T(8,128)S(1)}, f32[128,256]{1,0:T(8,128)S(1)}, u32[]{:S(2)}, u32[]{:S(2)}) %collective-permute-start.32) | collective-permute-done | bytes 131104 | tf_op jit(solution)/shard_map/ppermute | solution.py:150
  88.6 0.7 weight_halves.1
  89.3 0.8 total.1
  (33 shorter events, 0.2 us)
Async XLA Ops:
  0.6 14.4 %collective-permute-start.1 = (bf16[512,256]{1,0:T(8,128)(2,1)}, bf16[512,256]{1,0:T(8,128)(2,1)S(1)}, u32[]{:S(2)}, u32[]{:S(2)}) collective-permute-start(bf16[512,256]{1,0:T(8,128)(2,1)} %source_ref.1), channel_id=1, source_target_pairs={{0,16},{8,24},{16,0},{24,8},{1,17},{9,25},{17,1},{25,9},{2,18},{10... | collective-permute-start | bytes 786440 | tf_op jit(solution)/shard_map/ppermute | solution.py:150
  3.7 11.4 %collective-permute-start = (bf16[512,256]{1,0:T(8,128)(2,1)}, bf16[512,256]{1,0:T(8,128)(2,1)S(1)}, u32[]{:S(2)}, u32[]{:S(2)}) collective-permute-start(bf16[512,256]{1,0:T(8,128)(2,1)} %source_ref.1), channel_id=1, source_target_pairs={{0,8},{8,0},{16,24},{24,16},{1,9},{9,1},{17,25},{25,17},{2,10},{10... | collective-permute-start | bytes 786440 | tf_op jit(solution)/shard_map/ppermute | solution.py:150
  5.2 11.9 %collective-permute-start.2 = (bf16[512,256]{1,0:T(8,128)(2,1)}, bf16[512,256]{1,0:T(8,128)(2,1)S(1)}, u32[]{:S(2)}, u32[]{:S(2)}) collective-permute-start(bf16[512,256]{1,0:T(8,128)(2,1)} %source_ref.1), channel_id=1, source_target_pairs={{0,24},{8,16},{16,8},{24,0},{1,25},{9,17},{17,9},{25,1},{2,26},{10... | collective-permute-start | bytes 786440 | tf_op jit(solution)/shard_map/ppermute | solution.py:150
  5.9 8.0 %copy-start.2 = (bf16[512,256]{1,0:T(8,128)(2,1)S(1)}, bf16[512,256]{1,0:T(8,128)(2,1)}, u32[]{:S(2)}) copy-start(bf16[512,256]{1,0:T(8,128)(2,1)} %source_ref.1) | copy-start | bytes 786436
  18.0 1.6 %collective-permute-start.3 = (bf16[512,256]{1,0:T(8,128)(2,1)S(1)}, bf16[512,256]{1,0:T(8,128)(2,1)S(1)}, u32[]{:S(2)}, u32[]{:S(2)}) collective-permute-start(bf16[512,256]{1,0:T(8,128)(2,1)S(1)} %get-tuple-element.34), channel_id=1, source_target_pairs={{0,1},{1,0},{2,3},{3,2},{4,5},{5,4},{6,7},{7,6},{8,9},{9,8},{10,11... | collective-permute-start | bytes 786440 | tf_op jit(solution)/shard_map/ppermute | solution.py:150
  18.1 1.9 %collective-permute-start.4 = (bf16[512,256]{1,0:T(8,128)(2,1)S(1)}, bf16[512,256]{1,0:T(8,128)(2,1)S(1)}, u32[]{:S(2)}, u32[]{:S(2)}) collective-permute-start(bf16[512,256]{1,0:T(8,128)(2,1)S(1)} %get-tuple-element.35), channel_id=1, source_target_pairs={{0,1},{1,0},{2,3},{3,2},{4,5},{5,4},{6,7},{7,6},{8,9},{9,8},{10,11... | collective-permute-start | bytes 786440 | tf_op jit(solution)/shard_map/ppermute | solution.py:150
  20.1 21.4 %collective-permute-start.13 = (bf16[512,256]{1,0:T(8,128)(2,1)S(1)}, bf16[512,256]{1,0:T(8,128)(2,1)S(1)}, u32[]{:S(2)}, u32[]{:S(2)}) collective-permute-start(bf16[512,256]{1,0:T(8,128)(2,1)S(1)} %get-tuple-element.46), channel_id=1, source_target_pairs={{0,4},{1,5},{2,6},{3,7},{4,0},{5,1},{6,2},{7,3},{8,12},{9,13},{10,... | collective-permute-start | bytes 786440 | tf_op jit(solution)/shard_map/ppermute | solution.py:150
  22.9 18.6 %collective-permute-start.14 = (bf16[512,256]{1,0:T(8,128)(2,1)S(1)}, bf16[512,256]{1,0:T(8,128)(2,1)S(1)}, u32[]{:S(2)}, u32[]{:S(2)}) collective-permute-start(bf16[512,256]{1,0:T(8,128)(2,1)S(1)} %get-tuple-element.36.refs_5_), channel_id=1, source_target_pairs={{0,6},{1,7},{2,4},{3,5},{4,2},{5,3},{6,0},{7,1},{8,14},{9,15},{10,... | collective-permute-start | bytes 786440 | tf_op jit(solution)/shard_map/ppermute | solution.py:150
  25.3 1.3 %collective-permute-start.5 = (bf16[128,256]{1,0:T(8,128)(2,1)S(1)}, bf16[128,256]{1,0:T(8,128)(2,1)S(1)}, u32[]{:S(2)}, u32[]{:S(2)}) collective-permute-start(bf16[128,256]{1,0:T(8,128)(2,1)S(1)} %get-tuple-element.37), channel_id=1, source_target_pairs={{0,1},{1,0},{2,3},{3,2},{4,5},{5,4},{6,7},{7,6},{8,9},{9,8},{10,11... | collective-permute-start | bytes 196616 | tf_op jit(solution)/shard_map/ppermute | solution.py:150
  25.3 1.4 %collective-permute-start.6 = (bf16[128,256]{1,0:T(8,128)(2,1)S(1)}, bf16[128,256]{1,0:T(8,128)(2,1)S(1)}, u32[]{:S(2)}, u32[]{:S(2)}) collective-permute-start(bf16[128,256]{1,0:T(8,128)(2,1)S(1)} %get-tuple-element.38), channel_id=1, source_target_pairs={{0,1},{1,0},{2,3},{3,2},{4,5},{5,4},{6,7},{7,6},{8,9},{9,8},{10,11... | collective-permute-start | bytes 196616 | tf_op jit(solution)/shard_map/ppermute | solution.py:150
  25.8 1.3 %collective-permute-start.7 = (bf16[128,256]{1,0:T(8,128)(2,1)S(1)}, bf16[128,256]{1,0:T(8,128)(2,1)S(1)}, u32[]{:S(2)}, u32[]{:S(2)}) collective-permute-start(bf16[128,256]{1,0:T(8,128)(2,1)S(1)} %get-tuple-element.39), channel_id=1, source_target_pairs={{0,1},{1,0},{2,3},{3,2},{4,5},{5,4},{6,7},{7,6},{8,9},{9,8},{10,11... | collective-permute-start | bytes 196616 | tf_op jit(solution)/shard_map/ppermute | solution.py:150
  26.6 1.3 %collective-permute-start.8 = (bf16[128,256]{1,0:T(8,128)(2,1)S(1)}, bf16[128,256]{1,0:T(8,128)(2,1)S(1)}, u32[]{:S(2)}, u32[]{:S(2)}) collective-permute-start(bf16[128,256]{1,0:T(8,128)(2,1)S(1)} %get-tuple-element.40), channel_id=1, source_target_pairs={{0,1},{1,0},{2,3},{3,2},{4,5},{5,4},{6,7},{7,6},{8,9},{9,8},{10,11... | collective-permute-start | bytes 196616 | tf_op jit(solution)/shard_map/ppermute | solution.py:150
  26.7 1.3 %collective-permute-start.9 = (bf16[128,256]{1,0:T(8,128)(2,1)S(1)}, bf16[128,256]{1,0:T(8,128)(2,1)S(1)}, u32[]{:S(2)}, u32[]{:S(2)}) collective-permute-start(bf16[128,256]{1,0:T(8,128)(2,1)S(1)} %get-tuple-element.41), channel_id=1, source_target_pairs={{0,1},{1,0},{2,3},{3,2},{4,5},{5,4},{6,7},{7,6},{8,9},{9,8},{10,11... | collective-permute-start | bytes 196616 | tf_op jit(solution)/shard_map/ppermute | solution.py:150
  27.1 1.3 %collective-permute-start.10 = (bf16[128,256]{1,0:T(8,128)(2,1)S(1)}, bf16[128,256]{1,0:T(8,128)(2,1)S(1)}, u32[]{:S(2)}, u32[]{:S(2)}) collective-permute-start(bf16[128,256]{1,0:T(8,128)(2,1)S(1)} %get-tuple-element.42), channel_id=1, source_target_pairs={{0,1},{1,0},{2,3},{3,2},{4,5},{5,4},{6,7},{7,6},{8,9},{9,8},{10,11... | collective-permute-start | bytes 196616 | tf_op jit(solution)/shard_map/ppermute | solution.py:150
  27.8 1.3 %collective-permute-start.11 = (bf16[128,256]{1,0:T(8,128)(2,1)S(1)}, bf16[128,256]{1,0:T(8,128)(2,1)S(1)}, u32[]{:S(2)}, u32[]{:S(2)}) collective-permute-start(bf16[128,256]{1,0:T(8,128)(2,1)S(1)} %get-tuple-element.43), channel_id=1, source_target_pairs={{0,1},{1,0},{2,3},{3,2},{4,5},{5,4},{6,7},{7,6},{8,9},{9,8},{10,11... | collective-permute-start | bytes 196616 | tf_op jit(solution)/shard_map/ppermute | solution.py:150
  28.0 1.3 %collective-permute-start.12 = (bf16[128,256]{1,0:T(8,128)(2,1)S(1)}, bf16[128,256]{1,0:T(8,128)(2,1)S(1)}, u32[]{:S(2)}, u32[]{:S(2)}) collective-permute-start(bf16[128,256]{1,0:T(8,128)(2,1)S(1)} %get-tuple-element.44), channel_id=1, source_target_pairs={{0,1},{1,0},{2,3},{3,2},{4,5},{5,4},{6,7},{7,6},{8,9},{9,8},{10,11... | collective-permute-start | bytes 196616 | tf_op jit(solution)/shard_map/ppermute | solution.py:150
  30.2 13.4 %collective-permute-start.15 = (bf16[256,256]{1,0:T(8,128)(2,1)S(1)}, bf16[256,256]{1,0:T(8,128)(2,1)S(1)}, u32[]{:S(2)}, u32[]{:S(2)}) collective-permute-start(bf16[256,256]{1,0:T(8,128)(2,1)S(1)} %get-tuple-element.47), channel_id=1, source_target_pairs={{0,2},{1,3},{2,0},{3,1},{4,6},{5,7},{6,4},{7,5},{8,10},{9,11},{10,... | collective-permute-start | bytes 393224 | tf_op jit(solution)/shard_map/ppermute | solution.py:150
  30.5 15.8 %copy-start = (bf16[256,256]{1,0:T(8,128)(2,1)S(1)}, bf16[256,256]{1,0:T(8,128)(2,1)}, u32[]{:S(2)}) copy-start(bf16[256,256]{1,0:T(8,128)(2,1)} %weight_ref.3) | copy-start | bytes 393220
  30.5 15.8 %copy-start.1 = (bf16[512,256]{1,0:T(8,128)(2,1)S(1)}, bf16[512,256]{1,0:T(8,128)(2,1)}, u32[]{:S(2)}) copy-start(bf16[512,256]{1,0:T(8,128)(2,1)} %cotangent_ref.1) | copy-start | bytes 786436
  30.5 15.8 %collective-permute-start.16 = (bf16[256,256]{1,0:T(8,128)(2,1)S(1)}, bf16[256,256]{1,0:T(8,128)(2,1)S(1)}, u32[]{:S(2)}, u32[]{:S(2)}) collective-permute-start(bf16[256,256]{1,0:T(8,128)(2,1)S(1)} %get-tuple-element.48), channel_id=1, source_target_pairs={{0,2},{1,3},{2,0},{3,1},{4,6},{5,7},{6,4},{7,5},{8,10},{9,11},{10,... | collective-permute-start | bytes 393224 | tf_op jit(solution)/shard_map/ppermute | solution.py:150
  46.9 16.0 %collective-permute-start.18 = (bf16[512,256]{1,0:T(8,128)(2,1)S(1)}, bf16[512,256]{1,0:T(8,128)(2,1)S(1)}, u32[]{:S(2)}, u32[]{:S(2)}) collective-permute-start(bf16[512,256]{1,0:T(8,128)(2,1)S(1)} %get-tuple-element.52.refs_0_), channel_id=1, source_target_pairs={{0,2},{1,3},{2,0},{3,1},{4,6},{5,7},{6,4},{7,5},{8,10},{9,11},{10,... | collective-permute-start | bytes 786440 | tf_op jit(solution)/shard_map/ppermute | solution.py:150
  47.8 15.0 %collective-permute-start.17 = (bf16[512,256]{1,0:T(8,128)(2,1)S(1)}, bf16[512,256]{1,0:T(8,128)(2,1)S(1)}, u32[]{:S(2)}, u32[]{:S(2)}) collective-permute-start(bf16[512,256]{1,0:T(8,128)(2,1)S(1)} %get-tuple-element.52.refs_0_), channel_id=1, source_target_pairs={{0,1},{1,0},{2,3},{3,2},{4,5},{5,4},{6,7},{7,6},{8,9},{9,8},{10,11... | collective-permute-start | bytes 786440 | tf_op jit(solution)/shard_map/ppermute | solution.py:150
  47.8 21.7 %collective-permute-start.21 = (bf16[512,256]{1,0:T(8,128)(2,1)S(1)}, bf16[512,256]{1,0:T(8,128)(2,1)S(1)}, u32[]{:S(2)}, u32[]{:S(2)}) collective-permute-start(bf16[512,256]{1,0:T(8,128)(2,1)S(1)} %get-tuple-element.52.refs_0_), channel_id=1, source_target_pairs={{0,4},{1,5},{2,6},{3,7},{4,0},{5,1},{6,2},{7,3},{8,12},{9,13},{10,... | collective-permute-start | bytes 786440 | tf_op jit(solution)/shard_map/ppermute | solution.py:150
  51.0 18.5 %collective-permute-start.20 = (bf16[512,256]{1,0:T(8,128)(2,1)S(1)}, bf16[512,256]{1,0:T(8,128)(2,1)S(1)}, u32[]{:S(2)}, u32[]{:S(2)}) collective-permute-start(bf16[512,256]{1,0:T(8,128)(2,1)S(1)} %get-tuple-element.52.refs_0_), channel_id=1, source_target_pairs={{0,6},{1,7},{2,4},{3,5},{4,2},{5,3},{6,0},{7,1},{8,14},{9,15},{10,... | collective-permute-start | bytes 786440 | tf_op jit(solution)/shard_map/ppermute | solution.py:150
  52.4 1.3 %collective-permute-start.22 = (bf16[128,256]{1,0:T(8,128)(2,1)S(1)}, bf16[128,256]{1,0:T(8,128)(2,1)S(1)}, u32[]{:S(2)}, u32[]{:S(2)}) collective-permute-start(bf16[128,256]{1,0:T(8,128)(2,1)S(1)} %get-tuple-element.56), channel_id=1, source_target_pairs={{0,1},{1,0},{2,3},{3,2},{4,5},{5,4},{6,7},{7,6},{8,9},{9,8},{10,11... | collective-permute-start | bytes 196616 | tf_op jit(solution)/shard_map/ppermute | solution.py:150
  53.6 4.3 %collective-permute-start.23 = (bf16[128,256]{1,0:T(8,128)(2,1)S(1)}, bf16[128,256]{1,0:T(8,128)(2,1)S(1)}, u32[]{:S(2)}, u32[]{:S(2)}) collective-permute-start(bf16[128,256]{1,0:T(8,128)(2,1)S(1)} %weight_sum.5.mine_ref), channel_id=1, source_target_pairs={{0,8},{8,0},{16,24},{24,16},{1,9},{9,1},{17,25},{25,17},{2,10},{10... | collective-permute-start | bytes 196616 | tf_op jit(solution)/shard_map/ppermute | solution.py:150
  58.0 4.3 %collective-permute-start.24 = (bf16[128,256]{1,0:T(8,128)(2,1)S(1)}, bf16[128,256]{1,0:T(8,128)(2,1)S(1)}, u32[]{:S(2)}, u32[]{:S(2)}) collective-permute-start(bf16[128,256]{1,0:T(8,128)(2,1)S(1)} %weight_sum.6.mine_ref), channel_id=1, source_target_pairs={{0,16},{8,24},{16,0},{24,8},{1,17},{9,25},{17,1},{25,9},{2,18},{10... | collective-permute-start | bytes 196616 | tf_op jit(solution)/shard_map/ppermute | solution.py:150
  62.4 8.1 %collective-permute-start.25 = (bf16[128,256]{1,0:T(8,128)(2,1)S(1)}, bf16[128,256]{1,0:T(8,128)(2,1)S(1)}, u32[]{:S(2)}, u32[]{:S(2)}) collective-permute-start(bf16[128,256]{1,0:T(8,128)(2,1)S(1)} %weight_sum.7.mine_ref), channel_id=1, source_target_pairs={{0,2},{1,3},{2,0},{3,1},{4,6},{5,7},{6,4},{7,5},{8,10},{9,11},{10,... | collective-permute-start | bytes 196616 | tf_op jit(solution)/shard_map/ppermute | solution.py:150
  62.8 8.2 %collective-permute-start.19 = (bf16[512,256]{1,0:T(8,128)(2,1)S(1)}, bf16[512,256]{1,0:T(8,128)(2,1)S(1)}, u32[]{:S(2)}, u32[]{:S(2)}) collective-permute-start(bf16[512,256]{1,0:T(8,128)(2,1)S(1)} %collective-permute-done.18.refs_2_), channel_id=1, source_target_pairs={{0,1},{1,0},{2,3},{3,2},{4,5},{5,4},{6,7},{7,6},{8,9},{9,8},{10,11... | collective-permute-start | bytes 786440 | tf_op jit(solution)/shard_map/ppermute | solution.py:150
  70.4 2.5 %collective-permute-start.26 = (bf16[512,256]{1,0:T(8,128)(2,1)S(1)}, bf16[512,256]{1,0:T(8,128)(2,1)S(1)}, u32[]{:S(2)}, u32[]{:S(2)}) collective-permute-start(bf16[512,256]{1,0:T(8,128)(2,1)S(1)} %get-tuple-element.57.refs_1_), channel_id=1, source_target_pairs={{0,1},{1,0},{2,3},{3,2},{4,5},{5,4},{6,7},{7,6},{8,9},{9,8},{10,11... | collective-permute-start | bytes 786440 | tf_op jit(solution)/shard_map/ppermute | solution.py:150
  70.5 2.4 %collective-permute-start.27 = (bf16[512,256]{1,0:T(8,128)(2,1)S(1)}, bf16[512,256]{1,0:T(8,128)(2,1)S(1)}, u32[]{:S(2)}, u32[]{:S(2)}) collective-permute-start(bf16[512,256]{1,0:T(8,128)(2,1)S(1)} %get-tuple-element.58.refs_2_), channel_id=1, source_target_pairs={{0,1},{1,0},{2,3},{3,2},{4,5},{5,4},{6,7},{7,6},{8,9},{9,8},{10,11... | collective-permute-start | bytes 786440 | tf_op jit(solution)/shard_map/ppermute | solution.py:150
  73.4 15.8 %collective-permute-start.28 = (bf16[512,256]{1,0:T(8,128)(2,1)S(1)}, bf16[512,256]{1,0:T(8,128)(2,1)S(1)}, u32[]{:S(2)}, u32[]{:S(2)}) collective-permute-start(bf16[512,256]{1,0:T(8,128)(2,1)S(1)} %backward_far_away.2.refs_4_), channel_id=1, source_target_pairs={{0,24},{8,16},{16,8},{24,0},{1,25},{9,17},{17,9},{25,1},{2,26},{10... | collective-permute-start | bytes 786440 | tf_op jit(solution)/shard_map/ppermute | solution.py:150
  76.8 12.5 %collective-permute-start.29 = (bf16[512,256]{1,0:T(8,128)(2,1)S(1)}, bf16[512,256]{1,0:T(8,128)(2,1)S(1)}, u32[]{:S(2)}, u32[]{:S(2)}) collective-permute-start(bf16[512,256]{1,0:T(8,128)(2,1)S(1)} %get-tuple-element.59), channel_id=1, source_target_pairs={{0,16},{8,24},{16,0},{24,8},{1,17},{9,25},{17,1},{25,9},{2,18},{10... | collective-permute-start | bytes 786440 | tf_op jit(solution)/shard_map/ppermute | solution.py:150
  77.3 12.0 %collective-permute-start.30 = (bf16[512,256]{1,0:T(8,128)(2,1)S(1)}, bf16[512,256]{1,0:T(8,128)(2,1)S(1)}, u32[]{:S(2)}, u32[]{:S(2)}) collective-permute-start(bf16[512,256]{1,0:T(8,128)(2,1)S(1)} %get-tuple-element.60), channel_id=1, source_target_pairs={{0,8},{8,0},{16,24},{24,16},{1,9},{9,1},{17,25},{25,17},{2,10},{10... | collective-permute-start | bytes 786440 | tf_op jit(solution)/shard_map/ppermute | solution.py:150
  78.4 8.8 %collective-permute-start.31 = (bf16[128,256]{1,0:T(8,128)(2,1)S(1)}, bf16[128,256]{1,0:T(8,128)(2,1)S(1)}, u32[]{:S(2)}, u32[]{:S(2)}) collective-permute-start(bf16[128,256]{1,0:T(8,128)(2,1)S(1)} %later.5.mine_ref), channel_id=1, source_target_pairs={{0,4},{1,5},{2,6},{3,7},{4,0},{5,1},{6,2},{7,3},{8,12},{9,13},{10,... | collective-permute-start | bytes 196616 | tf_op jit(solution)/shard_map/ppermute | solution.py:150
  87.1 1.4 %collective-permute-start.32 = (f32[128,256]{1,0:T(8,128)S(1)}, f32[128,256]{1,0:T(8,128)S(1)}, u32[]{:S(2)}, u32[]{:S(2)}) collective-permute-start(f32[128,256]{1,0:T(8,128)S(1)} %weight_sum.9.half_ref), channel_id=1, source_target_pairs={{0,1},{1,0},{2,3},{3,2},{4,5},{5,4},{6,7},{7,6},{8,9},{9,8},{10,11... | collective-permute-start | bytes 393224 | tf_op jit(solution)/shard_map/ppermute | solution.py:150
